TPU v7x, 512 devices: a whole 4x4x16 slice. The times are simulated.
512 devices in a mesh: row: 32 (over z_lo, x), col: 16 (over y, z_hi, core).
Axes of the slice: x: 4, y: 4, z: 16 (z_hi: 2, z_lo: 8; z = z_hi * 8 + z_lo), core: 2. Of those that a mesh axis runs over, the one named last changes fastest.
Arguments:
- temp_in: float32 [2304, 16, 4608], P('row', 'col'), may hold values from -6 to 6
- velocity: bfloat16 [3, 16, 4608, 1536], P(None, 'col', 'row'), may hold values from -3 to 3
- spacing_x: float32 [1536], replicated, may hold values from 0.3 to 3
- inverse_x: float32 [12, 128, 128], replicated
- link_x: float32 [11], replicated, may hold values from 0.3 to 1.5
- inverse_z: float32 [36, 128, 128], replicated
- link_z: float32 [35], replicated, may hold values from 0.3 to 1.5
- counts_in: int32 [32], replicated, may hold values from 1 to 72, 1536 in all
- counts_out: int32 [32], replicated, may hold values from 1 to 72, 1536 in all
Outputs:
- temp_out: float32 [2304, 16, 4608], P('row', 'col')
Inputs may be any that keep to these rules, and one draw needn't show every extreme that they name: counts_in sums to 1536; some entry equals 72. counts_out sums to 1536; some entry equals 72.
All inputs are finite; a program needn't handle non-finite values.
Results may differ from a plain program's by a relative error of at most 0.0003.
Values sent between devices are 32-bit elements; how exact they have to be, the bound alone decides.
A program may use at most 64 MiB of HBM per device.

v0:
```python
import jax
import jax.numpy as jnp
from jax import lax
from jax.sharding import PartitionSpec as P


def padded_2(block, sides, width):
    for axis, dim in sides:
        count = lax.axis_size(axis)
        forward = [(i, i + 1) for i in range(count - 1)]
        forward.append((count - 1, 0))
        backward = [(target, source) for source, target in forward]
        low = lax.ppermute(
            lax.slice_in_dim(block, block.shape[dim] - width, None, axis=dim), axis, forward
        )
        high = lax.ppermute(lax.slice_in_dim(block, 0, width, axis=dim), axis, backward)
        block = jnp.concatenate([low, block, high], axis=dim)
    return block


def slot_positions(counts, slot_count, planes):
    slot_ends = jnp.cumsum(counts)
    slot_starts = slot_ends - counts
    owner_row = jnp.sum((planes[:, None] >= slot_ends[None, :]).astype(jnp.int32), axis=1)
    member = jnp.arange(counts.shape[0], dtype=jnp.int32)[None, :] == owner_row[:, None]
    start_of = jnp.sum(jnp.where(member, slot_starts[None, :], 0), axis=1)
    return owner_row * slot_count + planes - start_of


def exit_planes(counts, slot_count, plane_count):
    slots = jnp.arange(counts.shape[0] * slot_count, dtype=jnp.int32)
    owner_col = slots // slot_count
    within = slots % slot_count
    slot_starts = jnp.cumsum(counts) - counts
    member = jnp.arange(counts.shape[0], dtype=jnp.int32)[None, :] == owner_col[:, None]
    start_of = jnp.sum(jnp.where(member, slot_starts[None, :], 0), axis=1)
    count_of = jnp.sum(jnp.where(member, counts[None, :], 0), axis=1)
    valid = within < count_of
    target = jnp.minimum(start_of + within, plane_count - 1)
    return (target, valid)


def linear_scan(coef, values, reverse):

    def combine(earlier, later):
        return (earlier[0] * later[0], later[0] * earlier[1] + later[1])

    return lax.associative_scan(combine, (coef, values), reverse=reverse, axis=values.ndim - 1)[1]


def chain_solve(rhs, inverse, link):
    high = lax.Precision.HIGHEST
    solved = jnp.einsum("...kb,kmb->...km", rhs, inverse, precision=high)
    zero = jnp.zeros_like(link[:1])
    lower = jnp.concatenate([zero, link])
    upper = jnp.concatenate([link, zero])
    fwd_coef = jnp.broadcast_to(lower * inverse[:, -1, 0], solved.shape[:-1])
    ends = linear_scan(fwd_coef, solved[..., -1], False)
    before = jnp.concatenate([jnp.zeros_like(ends[..., :1]), ends[..., :-1]], axis=-1)
    forward = solved + lower[:, None] * inverse[:, :, 0] * before[..., None]
    back_coef = jnp.broadcast_to(upper * inverse[:, 0, -1], solved.shape[:-1])
    heads = linear_scan(back_coef, forward[..., 0], True)
    after = jnp.concatenate([heads[..., 1:], jnp.zeros_like(heads[..., :1])], axis=-1)
    return forward + upper[:, None] * inverse[:, :, -1] * after[..., None]


def on_device(
    temp_in, velocity, spacing_x, inverse_x, link_x, inverse_z, link_z, counts_in, counts_out
):
    plane_total = velocity.shape[3]
    block_size = inverse_x.shape[1]
    slot_in = temp_in.shape[0]
    slot_out = 3 * plane_total // (2 * lax.axis_size("row"))
    received = lax.all_to_all(temp_in, "row", split_axis=2, concat_axis=0, tiled=True)
    planes = jnp.arange(plane_total, dtype=jnp.int32)
    slot_index = slot_positions(counts_in, slot_in, planes)
    field = jnp.transpose(jnp.take(received, slot_index, axis=0), (1, 2, 0))
    padded = padded_2(field, (("row", 1), ("col", 0)), 1)
    flow_f = velocity.astype(jnp.float32)
    wall_pad = jnp.pad(field, ((0, 0), (0, 0), (1, 1)))
    grad_x = (wall_pad[:, :, 2:] - wall_pad[:, :, :-2]) * spacing_x[None, None, :]
    grad_y = padded[2:, 1:-1] - padded[:-2, 1:-1]
    grad_z = padded[1:-1, 2:] - padded[1:-1, :-2]
    advection = flow_f[0] * grad_x + 0.5 * (flow_f[1] * grad_y) + 0.5 * (flow_f[2] * grad_z)
    right_side = field - advection
    y_local, z_local = (right_side.shape[0], right_side.shape[1])
    lines_x = right_side.reshape(y_local, z_local, inverse_x.shape[0], block_size)
    after_x = chain_solve(lines_x, inverse_x, link_x).reshape(y_local, z_local, plane_total)
    target, valid = exit_planes(counts_out, slot_out, plane_total)
    picked = jnp.take(after_x, target, axis=2)
    outgoing = jnp.where(valid[None, None, :], picked, jnp.zeros_like(picked))
    z_lines = lax.all_to_all(outgoing, "row", split_axis=2, concat_axis=1, tiled=True)
    lines_z = jnp.transpose(z_lines, (2, 0, 1))
    slot_here, z_total = (lines_z.shape[0], lines_z.shape[2])
    stacked = lines_z.reshape(slot_here, y_local, inverse_z.shape[0], block_size)
    return chain_solve(stacked, inverse_z, link_z).reshape(slot_here, y_local, z_total)


def solution(mesh):
    in_specs = (
        P("row", "col", None),
        P(None, "col", "row", None),
        P(),
        P(),
        P(),
        P(),
        P(),
        P(),
        P(),
    )
    out_specs = P("row", "col", None)
    return jax.shard_map(
        on_device, mesh=mesh, in_specs=in_specs, out_specs=out_specs, check_vma=False
    )
```

profile of v0, /device:TPU:1, one launch (start us, length us, event | category | flops | bytes accessed | tf_op | source)
XLA Modules:
  0.0 448.6 jit_solution(13078457903551863683)
XLA Ops:
  0.0 8.0 %copy.115 = f32[72,1,4608]{0,1,2:T(1,128)} copy(f32[72,1,4608]{2,1,0:T(1,128)} %param.9) | data formatting | bytes 2654208 | tf_op args[0]
  8.0 16.1 %all-to-all-start = ((f32[72,1,4608]{0,1,2:T(1,128)}), f32[72,1,4608]{0,1,2:T(1,128)S(1)}, u32[]{:S(2)}, u32[]{:S(2)}) async-start(f32[72,1,4608]{0,1,2:T(1,128)} %copy.115), calls=%async_computation | async-start | bytes 4718592 | tf_op jit(solution)/shard_map/all_to_all | solution.py:74
  24.9 1.4 fusion.42
  26.3 103.8 %all-to-all-done = f32[72,1,4608]{0,1,2:T(1,128)S(1)} async-done(((f32[72,1,4608]{0,1,2:T(1,128)}), f32[72,1,4608]{0,1,2:T(1,128)S(1)}, u32[]{:S(2)}, u32[]{:S(2)}) %all-to-all-start) | async-done | bytes 1327136 | tf_op jit(solution)/shard_map/all_to_all | solution.py:74
  130.1 3.0 copy.142
  133.1 3.0 copy.117
  136.1 4.7 %gather_fusion = f32[1536,144]{1,0:T(8,128)} fusion(f32[2304,144]{1,0:T(8,128)S(1)} %bitcast.95, s32[2048]{0:T(1024)S(1)} %pad_clamp_fusion.1), kind=kCustom, calls=%fused_computation | custom fusion | bytes 1775616 | tf_op jit(solution)/shard_map/jit(_take)/gather | solution.py:77
  140.8 1.7 fusion.10
  142.4 1.2 fusion.41
  143.6 1.4 copy.119
  145.0 2.9 collective-permute-start
  148.1 11.1 %collective-permute-start.1 = (f32[1,1,1536]{2,1,0:T(1,128)S(1)}, f32[1,1,1536]{2,1,0:T(1,128)S(1)}, u32[]{:S(2)}, u32[]{:S(2)}) collective-permute-start(f32[1,1,1536]{2,1,0:T(1,128)S(1)} %copy.120), channel_id=1, source_target_pairs={{16,0},{32,16},{48,32},{64,48},{80,64},{96,80},{112,96},{128,112},... | collective-permute-start | bytes 18440 | tf_op jit(solution)/shard_map/ppermute | solution.py:16
  160.2 3.8 copy.118
  164.0 4.3 convert_element_type.9
  168.3 1.5 copy.152
  170.7 1.3 copy.122
  172.0 3.0 pad_maximum_fusion.2
  175.0 3.4 copy.123
  178.4 4.4 collective-permute-start.2
  182.8 10.0 %collective-permute-start.3 = (f32[1,146,1536]{2,0,1:T(1,128)}, f32[1,146,1536]{2,0,1:T(1,128)}, u32[]{:S(2)}, u32[]{:S(2)}) collective-permute-start(f32[1,146,1536]{2,0,1:T(1,128)} %copy.123), channel_id=1, source_target_pairs={{0,1},{1,2},{2,3},{3,4},{4,5},{5,6},{6,7},{7,8},{8,9},{9,10},{10,1... | collective-permute-start | bytes 2691080 | tf_op jit(solution)/shard_map/ppermute | solution.py:13
  193.9 46.0 %collective-permute-done.2 = f32[1,146,1536]{2,0,1:T(1,128)S(1)} collective-permute-done((f32[1,146,1536]{2,0,1:T(1,128)}, f32[1,146,1536]{2,0,1:T(1,128)S(1)}, u32[]{:S(2)}, u32[]{:S(2)}) %collective-permute-start.2) | collective-permute-done | bytes 897056 | tf_op jit(solution)/shard_map/ppermute | solution.py:16
  239.9 1.5 slice.679
  241.4 3.3 copy.149
  244.7 2.7 slice.680
  247.4 3.3 copy.150
  250.7 4.4 fusion.5
  255.1 2.6 convolution_bitcast_fusion.1
  257.7 0.8 slice_reduce_fusion.3
  258.7 1.3 slice_add_fusion.14
  263.1 6.5 %gather_fusion.1 = f32[2304,144]{1,0:T(8,128)} fusion(f32[144,1536]{0,1:T(8,128)S(1)} %bitcast.96, s32[3072]{0:T(1024)S(1)} %pad_clamp_fusion), kind=kCustom, calls=%fused_computation.1 | custom fusion | bytes 2663424 | tf_op jit(solution)/shard_map/jit(_take)/gather | solution.py:90
  269.6 3.4 fusion
  273.0 11.1 %copy.134 = f32[1,144,2304]{1,0,2:T(1,128)} copy(f32[1,144,2304]{1,2,0:T(8,128)S(1)} %fusion) | data formatting | bytes 2654208 | tf_op jit(solution)/shard_map/jit(_where)/select_n | solution.py:91
  284.1 31.3 %all-to-all-start.1 = ((f32[1,144,2304]{1,0,2:T(1,128)}), f32[1,144,2304]{1,0,2:T(1,128)}, u32[]{:S(2)}, u32[]{:S(2)}) async-start(f32[1,144,2304]{1,0,2:T(1,128)} %copy.134), calls=%async_computation.1 | async-start | bytes 4718592 | tf_op jit(solution)/shard_map/all_to_all | solution.py:92
  318.9 3.0 fusion.40
  321.9 2.4 copy.154
  324.3 2.4 copy.153
  326.9 92.8 %all-to-all-done.1 = f32[1,144,2304]{1,0,2:T(1,128)} async-done(((f32[1,144,2304]{1,0,2:T(1,128)}), f32[1,144,2304]{1,0,2:T(1,128)}, u32[]{:S(2)}, u32[]{:S(2)}) %all-to-all-start.1) | async-done | bytes 1327136 | tf_op jit(solution)/shard_map/all_to_all | solution.py:92
  419.7 3.8 copy.162
  423.5 3.6 all_to_all.33
  427.1 2.5 reshape.371
  429.6 6.4 %convolution_bitcast_fusion = f32[72,1,36,128]{3,0,2,1:T(8,128)S(1)} fusion(f32[36,128,128]{2,1,0:T(8,128)S(1)} %copy-done, f32[72,36,128]{2,1,0:T(8,128)} %reshape.371), kind=kOutput, calls=%fused_computation.22 | convolution fusion | flops 509607936 | bytes 5013504 | tf_op jit(solution)/shard_map/...kb,kmb->...km/dot_general | solution.py:53
  436.0 1.1 copy-done.1
  437.1 1.0 slice_reduce_fusion.1
  438.5 0.7 fusion.49
  441.1 1.7 multiply_add_fusion.1
  442.8 0.7 slice_reduce_fusion
  445.0 0.9 multiply_add_fusion
  446.3 2.4 reshape.395
  (201 shorter events, 14.3 us)
Async XLA Ops:
  8.0 16.1 %copy-start.7 = (s32[32]{0:T(128)S(1)}, s32[32]{0:T(128)}, u32[]{:S(2)}) copy-start(s32[32]{0:T(128)} %param.16) | copy-start | bytes 388
  8.0 16.6 %copy-start.3 = (f32[12,128,128]{2,1,0:T(8,128)S(1)}, f32[12,128,128]{2,1,0:T(8,128)}, u32[]{:S(2)}) copy-start(f32[12,128,128]{2,1,0:T(8,128)} %param.12) | copy-start | bytes 2359300
  8.0 122.1 %all-to-all-start = ((f32[72,1,4608]{0,1,2:T(1,128)}), f32[72,1,4608]{0,1,2:T(1,128)S(1)}, u32[]{:S(2)}, u32[]{:S(2)}) async-start(f32[72,1,4608]{0,1,2:T(1,128)} %copy.115), calls=%async_computation | async-start | bytes 4718592 | tf_op jit(solution)/shard_map/all_to_all | solution.py:74
  143.6 15.7 %copy-start.8 = (f32[11]{0:T(128)S(1)}, f32[11]{0:T(128)}, u32[]{:S(2)}) copy-start(f32[11]{0:T(128)} %param.13) | copy-start | bytes 136
  145.0 25.4 %collective-permute-start = (f32[1,1,1536]{2,1,0:T(1,128)S(1)}, f32[1,1,1536]{2,1,0:T(1,128)S(1)}, u32[]{:S(2)}, u32[]{:S(2)}) collective-permute-start(f32[1,1,1536]{2,1,0:T(1,128)S(1)} %copy.119), channel_id=1, source_target_pairs={{0,16},{16,32},{32,48},{48,64},{64,80},{80,96},{96,112},{112,128},... | collective-permute-start | bytes 18440 | tf_op jit(solution)/shard_map/ppermute | solution.py:13
  148.1 22.6 %collective-permute-start.1 = (f32[1,1,1536]{2,1,0:T(1,128)S(1)}, f32[1,1,1536]{2,1,0:T(1,128)S(1)}, u32[]{:S(2)}, u32[]{:S(2)}) collective-permute-start(f32[1,1,1536]{2,1,0:T(1,128)S(1)} %copy.120), channel_id=1, source_target_pairs={{16,0},{32,16},{48,32},{64,48},{80,64},{96,80},{112,96},{128,112},... | collective-permute-start | bytes 18440 | tf_op jit(solution)/shard_map/ppermute | solution.py:16
  164.0 5.7 %copy-start.4 = (f32[12,128,1]{2,1,0:T(8,128)S(1)}, f32[12,128,1]{2,1,0:T(8,128)}, u32[]{:S(2)}) copy-start(f32[12,128,1]{2,1,0:T(8,128)} %get-tuple-element.24) | copy-start | bytes 18436
  168.3 1.8 copy-start.6
  178.4 61.5 %collective-permute-start.2 = (f32[1,146,1536]{2,0,1:T(1,128)}, f32[1,146,1536]{2,0,1:T(1,128)S(1)}, u32[]{:S(2)}, u32[]{:S(2)}) collective-permute-start(f32[1,146,1536]{2,0,1:T(1,128)} %copy.123), channel_id=1, source_target_pairs={{1,0},{2,1},{3,2},{4,3},{5,4},{6,5},{7,6},{8,7},{9,8},{10,9},{11,1... | collective-permute-start | bytes 2691080 | tf_op jit(solution)/shard_map/ppermute | solution.py:16
  182.8 61.9 %collective-permute-start.3 = (f32[1,146,1536]{2,0,1:T(1,128)}, f32[1,146,1536]{2,0,1:T(1,128)}, u32[]{:S(2)}, u32[]{:S(2)}) collective-permute-start(f32[1,146,1536]{2,0,1:T(1,128)} %copy.123), channel_id=1, source_target_pairs={{0,1},{1,2},{2,3},{3,4},{4,5},{5,6},{6,7},{7,8},{8,9},{9,10},{10,1... | collective-permute-start | bytes 2691080 | tf_op jit(solution)/shard_map/ppermute | solution.py:13
  247.4 3.3 copy-start.5
  284.1 31.3 %copy-start = (f32[36,128,128]{2,1,0:T(8,128)S(1)}, f32[36,128,128]{2,1,0:T(8,128)}, u32[]{:S(2)}) copy-start(f32[36,128,128]{2,1,0:T(8,128)} %param.14) | copy-start | bytes 7077892
  284.1 31.9 %copy-start.9 = (f32[35]{0:T(128)S(1)}, f32[35]{0:T(128)}, u32[]{:S(2)}) copy-start(f32[35]{0:T(128)} %param.15) | copy-start | bytes 424
  284.1 135.6 %all-to-all-start.1 = ((f32[1,144,2304]{1,0,2:T(1,128)}), f32[1,144,2304]{1,0,2:T(1,128)}, u32[]{:S(2)}, u32[]{:S(2)}) async-start(f32[1,144,2304]{1,0,2:T(1,128)} %copy.134), calls=%async_computation.1 | async-start | bytes 4718592 | tf_op jit(solution)/shard_map/all_to_all | solution.py:92
  436.0 1.1 copy-start.1
  442.8 2.2 copy-start.2
where the time goes:
time: 450 us; the launch traced here: 449 us
  waiting for transfers between devices  243 us (54%)
  local copies, waits for them, and re-layouts  95 us (21%)
  starting transfers between devices  75.8 us (17%)
  other arithmetic  25.3 us (6%)
  matrix products  9.02 us (2%)
    all_to_all x1, waiting for transfers between devices, on_device(): lax.all_to_all(temp_in, 'row', split_axis=2, concat_axis=0, tiled=True)  104 us
    all_to_all x1, waiting for transfers between devices, on_device(): lax.all_to_all(outgoing, 'row', split_axis=2, concat_axis=1, tiled=True)  92.8 us
    ppermute x2, waiting for transfers between devices, padded_2(): lax.ppermute(lax.slice_in_dim(block, 0, width, axis=dim), axis, backward)  46 us
    all_to_all x1, starting transfers between devices, on_device(): lax.all_to_all(outgoing, 'row', split_axis=2, concat_axis=1, tiled=True)  31.3 us
    unnamed x40, local copies, waits for them, and re-layouts  26.9 us
    all_to_all x1, starting transfers between devices, on_device(): lax.all_to_all(temp_in, 'row', split_axis=2, concat_axis=0, tiled=True)  16.1 us
    ppermute x2, starting transfers between devices, padded_2(): lax.ppermute(lax.slice_in_dim(block, 0, width, axis=dim), axis, backward)  15.5 us
    ppermute x2, starting transfers between devices, padded_2(): lax.ppermute(lax.slice_in_dim(block, block.shape[dim] - width, None, axis...  12.9 us
  transfers between devices with their start and end apart: 6, of which 3 were waited for; matrix products, arithmetic and copies ran while one was open for 7% of the time, Pallas kernels for 0%

commit v1 on v0

v1 whole, which is shorter than its diff:
```python
import functools
import jax
import jax.numpy as jnp
from jax import lax
from jax.experimental import pallas as pl
from jax.experimental.pallas import tpu as pltpu
from jax.sharding import PartitionSpec as P

MESH = pl.DeviceIdType.MESH
HIGH = lax.Precision.HIGH
B = 128
NQ = 8
QX = 4
ZL = 144
SLOTS = 72
KX = 12
KZ = 36
NT = 3
HALO = 8
FIELD_TILES = KX + NT
F32 = jnp.float32
LIMIT = 48 * 2**20


def here():
    row = lax.axis_index("row")
    return row // QX, row % QX, lax.axis_index("col")


def prefix(counts, first, number):
    total = jnp.int32(0)
    for i in range(number):
        total = total + counts[first + i]
    return total


def quad_starts(counts):
    starts, total = [], jnp.int32(0)
    for q in range(NQ):
        starts.append(total)
        total = total + prefix(counts, QX * q, QX)
    return starts


def offsets(counts, q):
    out, total = [], jnp.int32(0)
    for i in range(QX):
        out.append(total)
        total = total + counts[QX * q + i]
    return out


def own_offset(counts, q, x):
    total = jnp.int32(0)
    for i in range(QX - 1):
        total = total + jnp.where(i < x, counts[QX * q + i], 0)
    return total


def turn_kernel(counts, temp, out):
    q, x, _ = here()
    shift = own_offset(counts, q, x) % B
    pad = jnp.zeros((B - SLOTS, B), F32)
    for k in range(KZ):
        block = temp[pl.ds(k, SLOTS, stride=KZ), :]
        turned = jnp.concatenate([block, pad], axis=0).T
        out[HALO + B * k : HALO + B * (k + 1), :] = pltpu.roll(turned, shift, 1)
    total = KZ * B
    out[0:HALO, :] = out[total : total + HALO, :]
    out[total + HALO : total + 2 * HALO, :] = out[HALO : 2 * HALO, :]


def across(c):
    return jnp.where(c % 2 == 1, (c + 1) % 16, (c + 15) % 16)


def barrier(partners):
    sem = pltpu.get_barrier_semaphore()
    for row, col in partners:
        pl.semaphore_signal(
            sem, inc=1, device_id={"row": row, "col": col}, device_id_type=MESH
        )
    pl.semaphore_wait(sem, len(partners))


def remote(src, dst, send, recv, row, col):
    return pltpu.make_async_remote_copy(
        src_ref=src,
        dst_ref=dst,
        send_sem=send,
        recv_sem=recv,
        device_id={"row": row, "col": col},
        device_id_type=MESH,
    )


ORDER = (7, 6, 5, 4, 3, 2, 1, 0)


def entry_kernel(
    tiles, counts, turned, own, cross, mate, xin, merged,
    x_send, x_recv, x_local, o_send, o_recv, c_send, c_recv, m_send, m_recv, o_local,
):
    q, x, c = here()
    other, twin = across(c), c + 1 - 2 * (c % 2)
    row = QX * q + x
    wide = tiles * B
    partners = [(QX * q + (x + s) % QX, c) for s in range(1, QX)]
    partners += [(QX * ((q + s) % NQ) + x, c) for s in range(1, NQ)]
    partners += [(QX * ((q + s) % NQ) + x, other) for s in range(NQ)]
    partners += [(row, twin)]
    barrier(partners)
    span = ZL + 2 * HALO

    def piece(to_q, to_x):
        start = pl.multiple_of(QX * ZL * to_q + ZL * to_x, 8)
        return turned.at[pl.ds(start, span), :]

    started = []
    x_copies = {}
    for s in ORDER:
        to_q = (q + s) % NQ
        local = pltpu.make_async_copy(piece(to_q, x), xin.at[x, s], x_local.at[s])
        local.start()
        copies = [local]
        for d in range(1, QX):
            to_x = (x + d) % QX
            cp = remote(
                piece(to_q, to_x), xin.at[x, s], x_send.at[d, s], x_recv.at[d, s],
                QX * q + to_x, c,
            )
            cp.start()
            copies.append(cp)
        x_copies[s] = copies
    offs = offsets(counts, q)
    cnts = [counts[QX * q + i] for i in range(QX)]
    lane = lax.broadcasted_iota(jnp.int32, (8, B), 1)
    sub = lax.broadcasted_iota(jnp.int32, (8, B), 0)
    takes = []
    for t in range(tiles):
        at = lane + B * t
        takes.append([(at >= offs[i]) & (at < offs[i] + cnts[i]) for i in range(QX)])
    o_copies, c_copies = {}, {}
    for s in ORDER:
        to_q = (q + s) % NQ
        x_copies[s][0].wait()
        for cp in x_copies[s][1:]:
            cp.wait_recv()

        def put(to_row, parts):
            for t in range(tiles):
                value = jnp.zeros((8, B), F32)
                for i in range(QX):
                    value = jnp.where(takes[t][i], parts[i], value)
                merged[s, pl.ds(to_row, 8), B * t : B * (t + 1)] = value

        def step(j, carry):
            r0 = pl.multiple_of(8 * j, 8)
            put(r0, [xin[i, s, pl.ds(r0 + HALO, 8), :] for i in range(QX)])
            return carry

        lax.fori_loop(0, ZL // 8, step, 0)
        put(
            ZL,
            [
                jnp.where(
                    sub == 7, xin[i, s, 0:HALO, :], xin[i, s, ZL + HALO : ZL + 2 * HALO, :]
                )
                for i in range(QX)
            ],
        )
        if s:
            cp = remote(
                merged.at[s, :, 0:wide], own.at[q, :, 0:wide], o_send.at[s], o_recv.at[s],
                QX * to_q + x, c,
            )
        else:
            cp = pltpu.make_async_copy(
                merged.at[s, :, 0:wide], own.at[q, :, 0:wide], o_local.at[0]
            )
        cp.start()
        o_copies[s] = cp
        cp = remote(
            merged.at[s, 0:ZL, 0:wide], cross.at[q, :, 0:wide], c_send.at[s], c_recv.at[s],
            QX * to_q + x, other,
        )
        cp.start()
        c_copies[s] = cp
    m_copies = {}
    for s in range(NQ):
        from_q = (q + NQ - s) % NQ
        if s:
            o_copies[s].wait_recv()
        else:
            o_copies[s].wait()
        cp = remote(
            own.at[from_q, 0:ZL, 0:wide], mate.at[from_q, :, 0:wide],
            m_send.at[s], m_recv.at[s], row, twin,
        )
        cp.start()
        m_copies[s] = cp
    for s in range(NQ):
        m_copies[s].wait()
        c_copies[s].wait()
        if s:
            o_copies[s].wait_send()
        for cp in x_copies[s][1:]:
            cp.wait_send()


def entry(tiles, cid, counts, turned):
    dma = pltpu.SemaphoreType.DMA
    span = ZL + 2 * HALO
    return pl.pallas_call(
        functools.partial(entry_kernel, tiles),
        name="entry%d" % tiles,
        out_shape=(
            jax.ShapeDtypeStruct((NQ, ZL + HALO, NT * B), F32),
            jax.ShapeDtypeStruct((NQ, ZL, NT * B), F32),
            jax.ShapeDtypeStruct((NQ, ZL, NT * B), F32),
        ),
        in_specs=[
            pl.BlockSpec(memory_space=pltpu.SMEM),
            pl.BlockSpec(memory_space=pltpu.VMEM),
        ],
        out_specs=[pl.BlockSpec(memory_space=pl.ANY)] * 3,
        scratch_shapes=[
            pltpu.VMEM((QX, NQ, span, B), F32),
            pltpu.VMEM((NQ, ZL + HALO, NT * B), F32),
            dma((QX, NQ)), dma((QX, NQ)), dma((NQ,)),
            dma((NQ,)), dma((NQ,)), dma((NQ,)), dma((NQ,)), dma((NQ,)), dma((NQ,)),
            dma((1,)),
        ],
        compiler_params=pltpu.CompilerParams(
            collective_id=cid, has_side_effects=True, vmem_limit_bytes=LIMIT
        ),
    )(counts, turned)


def middle_kernel(
    counts_in, counts_out, link, own, cross, mate, vel, spacing, inverse, out,
    field, diff, right, solved, coef,
):
    c = lax.axis_index("col")
    starts = quad_starts(counts_in)
    lane = lax.broadcasted_iota(jnp.int32, (1, B), 1)

    def place(dst, first, start, parts):
        shift = start % B
        base = pl.multiple_of(start - shift, B)
        keep = lane >= shift
        rolled = [pltpu.roll(part, shift, 1) for part in parts]
        rows = pl.ds(first, parts[0].shape[0])
        dst[rows, pl.ds(base, B)] = jnp.where(keep, rolled[0], dst[rows, pl.ds(base, B)])
        for t in range(1, NT):
            dst[rows, pl.ds(base + B * t, B)] = jnp.where(keep, rolled[t], rolled[t - 1])
        dst[rows, pl.ds(base + B * NT, B)] = rolled[NT - 1]

    sign = jnp.where(c % 2 == 0, F32(1), F32(-1))
    for q in range(NQ):
        place(field, HALO, starts[q], [own[q, :, B * t : B * (t + 1)] for t in range(NT)])
        place(
            diff,
            0,
            starts[q],
            [
                (mate[q, :, B * t : B * (t + 1)] - cross[q, :, B * t : B * (t + 1)]) * sign
                for t in range(NT)
            ],
        )
    field[HALO - 1 : HALO, :] = field[ZL + 2 * HALO - 1 : ZL + 2 * HALO, :]
    nx = KX * B
    step = 16
    at = lax.broadcasted_iota(jnp.int32, (step, nx), 1)
    scale = spacing[...]
    for i in range(ZL // step):
        r0 = HALO + step * i
        here_f = field[r0 : r0 + step, 0:nx]
        low = jnp.where(at == 0, 0.0, pltpu.roll(here_f, 1, 1))
        high = jnp.where(at == nx - 1, 0.0, pltpu.roll(here_f, nx - 1, 1))
        grad_z = field[r0 + 1 : r0 + 1 + step, 0:nx] - field[r0 - 1 : r0 - 1 + step, 0:nx]
        grad_y = diff[step * i : step * (i + 1), 0:nx]
        u, v, w = [vel[j, step * i : step * (i + 1), :].astype(F32) for j in range(3)]
        advection = u * ((high - low) * scale) + 0.5 * (v * grad_y) + 0.5 * (w * grad_z)
        right[step * i : step * (i + 1), :] = here_f - advection
    end = None
    for k in range(KX):
        turned = inverse[k].T
        y = jnp.dot(
            right[:, B * k : B * (k + 1)], turned, precision=HIGH, preferred_element_type=F32
        )
        if k:
            y = y + (link[k - 1] * turned[0:1, :]) * end
        if k < KX - 1:
            coef[k : k + 1, :] = link[k] * turned[B - 1 : B, :]
        end = y[:, B - 1 : B]
        solved[:, B * k : B * (k + 1)] = y
    head = None
    for k in reversed(range(KX)):
        y = solved[:, B * k : B * (k + 1)]
        if k < KX - 1:
            y = y + coef[k : k + 1, :] * head
            solved[:, B * k : B * (k + 1)] = y
        head = y[:, 0:1]
    goals = quad_starts(counts_out)
    for q in range(NQ):
        shift = goals[q] % B
        base = pl.multiple_of(goals[q] - shift, B)
        back = (B - shift) % B
        keep = lane < B - shift
        rolled = [
            pltpu.roll(solved[:, pl.ds(base + B * t, B)], back, 1) for t in range(NT + 1)
        ]
        for t in range(NT):
            out[q, :, B * t : B * (t + 1)] = jnp.where(keep, rolled[t], rolled[t + 1])


def middle(counts_in, counts_out, link, own, cross, mate, vel, spacing, inverse):
    vmem = pl.BlockSpec(memory_space=pltpu.VMEM)
    smem = pl.BlockSpec(memory_space=pltpu.SMEM)
    wide = FIELD_TILES * B
    return pl.pallas_call(
        middle_kernel,
        name="middle",
        out_shape=jax.ShapeDtypeStruct((NQ, ZL, NT * B), F32),
        in_specs=[smem] * 3 + [vmem] * 6,
        out_specs=vmem,
        scratch_shapes=[
            pltpu.VMEM((ZL + 2 * HALO, wide), F32),
            pltpu.VMEM((ZL, wide), F32),
            pltpu.VMEM((ZL, KX * B), F32),
            pltpu.VMEM((ZL, wide), F32),
            pltpu.VMEM((KX + 4, B), F32),
        ],
        compiler_params=pltpu.CompilerParams(vmem_limit_bytes=LIMIT),
    )(counts_in, counts_out, link, own, cross, mate, vel, spacing, inverse)


def exit_kernel(
    tiles, counts, packed, out, rz, piece,
    z_send, z_recv, x_send, x_recv, x_local,
):
    q, x, c = here()
    wide = tiles * B
    partners = [(QX * q + (x + s) % QX, c) for s in range(1, QX)]
    partners += [(QX * ((q + s) % NQ) + x, c) for s in range(1, NQ)]
    barrier(partners)
    z_copies = {}
    for s in range(NQ - 1, 0, -1):
        to_q = (q + s) % NQ
        cp = remote(
            packed.at[to_q, :, 0:wide], rz.at[q, :, 0:wide], z_send.at[s], z_recv.at[s],
            QX * to_q + x, c,
        )
        cp.start()
        z_copies[s] = cp
    offs = offsets(counts, q)
    lane = lax.broadcasted_iota(jnp.int32, (8, B), 1)
    x_copies = []
    for s in range(NQ):
        from_q = (q + NQ - s) % NQ
        if s:
            z_copies[s].wait_recv()
        for d in range(QX):
            to_x = (x + d) % QX
            off = own_offset(counts, q, to_x)
            takes = [(lane + B * t >= off) & (lane + B * t < off + B) for t in range(tiles)]

            def step(j, carry):
                rows = pl.ds(pl.multiple_of(8 * j, 8), 8)
                value = jnp.zeros((8, B), F32)
                for t in range(tiles):
                    cols = slice(B * t, B * (t + 1))
                    if s:
                        part = rz[from_q, rows, cols]
                    else:
                        part = packed[q, rows, cols]
                    value = jnp.where(takes[t], part, value)
                piece[d, s, rows, :] = value
                return carry

            lax.fori_loop(0, ZL // 8, step, 0)
            first = pl.multiple_of(ZL * (QX * from_q + x), 8)
            if d:
                cp = remote(
                    piece.at[d, s], out.at[pl.ds(first, ZL), :],
                    x_send.at[d, s], x_recv.at[d, s], QX * q + to_x, c,
                )
            else:
                cp = pltpu.make_async_copy(
                    piece.at[d, s], out.at[pl.ds(first, ZL), :], x_local.at[s]
                )
            cp.start()
            x_copies.append(cp)
    for cp in x_copies:
        cp.wait()
    for s in range(1, NQ):
        z_copies[s].wait_send()


def leave(tiles, cid, counts, packed):
    dma = pltpu.SemaphoreType.DMA
    return pl.pallas_call(
        functools.partial(exit_kernel, tiles),
        name="leave%d" % tiles,
        out_shape=jax.ShapeDtypeStruct((KZ * B, B), F32),
        in_specs=[
            pl.BlockSpec(memory_space=pltpu.SMEM),
            pl.BlockSpec(memory_space=pltpu.VMEM),
        ],
        out_specs=pl.BlockSpec(memory_space=pl.ANY),
        scratch_shapes=[
            pltpu.VMEM((NQ, ZL, NT * B), F32),
            pltpu.VMEM((QX, NQ, ZL, B), F32),
            dma((NQ,)), dma((NQ,)), dma((QX, NQ)), dma((QX, NQ)), dma((NQ,)),
        ],
        compiler_params=pltpu.CompilerParams(
            collective_id=cid, has_side_effects=True, vmem_limit_bytes=LIMIT
        ),
    )(counts, packed)


def last_kernel(counts, link, lines, inverse, out, solved):
    q, x, _ = here()
    off = own_offset(counts, q, x)
    back = (B - off % B) % B
    count = counts[QX * q + x]
    valid = lax.broadcasted_iota(jnp.int32, (SLOTS, B), 0) < count
    end = None
    for k in range(KZ):
        y = jnp.dot(
            inverse[k], lines[B * k : B * (k + 1), :], precision=HIGH,
            preferred_element_type=F32,
        )
        if k:
            y = y + (link[k - 1] * inverse[k, :, 0:1]) * end
        end = y[B - 1 : B, :]
        solved[B * k : B * (k + 1), :] = y
    head = None
    for k in reversed(range(KZ)):
        y = solved[B * k : B * (k + 1), :]
        if k < KZ - 1:
            y = y + (link[k] * inverse[k, :, B - 1 : B]) * head
        head = y[0:1, :]
        turned = pltpu.roll(y, back, 1).T
        out[pl.ds(k, SLOTS, stride=KZ), :] = jnp.where(valid, turned[0:SLOTS, :], 0.0)


def on_device(
    temp_in, velocity, spacing_x, inverse_x, link_x, inverse_z, link_z, counts_in, counts_out
):
    vmem = pl.BlockSpec(memory_space=pltpu.VMEM)
    smem = pl.BlockSpec(memory_space=pltpu.SMEM)
    local = pltpu.CompilerParams(vmem_limit_bytes=LIMIT)
    turned = pl.pallas_call(
        turn_kernel,
        name="turn",
        out_shape=jax.ShapeDtypeStruct((KZ * B + 2 * HALO, B), F32),
        in_specs=[smem, vmem],
        out_specs=vmem,
        compiler_params=local,
    )(counts_in, temp_in.reshape(SLOTS * KZ, B))
    fits_in = jnp.max(jnp.sum(counts_in.reshape(NQ, QX), axis=1)) <= 2 * B
    fits_out = jnp.max(jnp.sum(counts_out.reshape(NQ, QX), axis=1)) <= 2 * B
    own, cross, mate = lax.cond(
        fits_in,
        functools.partial(entry, 2, 1),
        functools.partial(entry, 3, 2),
        counts_in,
        turned,
    )
    packed = middle(
        counts_in, counts_out, link_x, own, cross, mate,
        velocity.reshape(3, ZL, KX * B), spacing_x.reshape(1, KX * B), inverse_x,
    )
    lines = lax.cond(
        fits_out,
        functools.partial(leave, 2, 3),
        functools.partial(leave, 3, 4),
        counts_out,
        packed,
    )
    out = pl.pallas_call(
        last_kernel,
        name="last",
        out_shape=jax.ShapeDtypeStruct((SLOTS * KZ, B), F32),
        in_specs=[smem, smem, vmem, vmem],
        out_specs=vmem,
        scratch_shapes=[pltpu.VMEM((KZ * B, B), F32)],
        compiler_params=local,
    )(counts_out, link_z, lines, inverse_z)
    return out.reshape(SLOTS, 1, KZ * B)


def solution(mesh):
    in_specs = (
        P("row", "col", None),
        P(None, "col", "row", None),
        P(),
        P(),
        P(),
        P(),
        P(),
        P(),
        P(),
    )
    out_specs = P("row", "col", None)
    return jax.shard_map(
        on_device, mesh=mesh, in_specs=in_specs, out_specs=out_specs, check_vma=False
    )
```

time: 450 us -> 261 us (0.58)
  the two profiles are of different devices: /device:TPU:1 before, /device:TPU:136 now
where the time goes in v1:
time: 261 us
  Pallas kernels  256 us (98%)
    pallas_call x1, Pallas kernels, entry(): pl.pallas_call(functools.partial(entry_kernel, tiles), name='entry%d' % t...  128 us
    pallas_call x1, Pallas kernels, leave(): pl.pallas_call(functools.partial(exit_kernel, tiles), name='leave%d' % ti...  110 us
    pallas_call x1, Pallas kernels, middle(): pl.pallas_call(middle_kernel, name='middle', out_shape=jax.ShapeDtypeStru...  8.01 us
    pallas_call x1, Pallas kernels, on_device(): pl.pallas_call(last_kernel, name='last', out_shape=jax.ShapeDtypeStruct((...  7 us

profile of v1, /device:TPU:136, one launch (start us, length us, event | category | flops | bytes accessed | tf_op | source)
XLA Modules:
  0.0 260.9 jit_solution(16514351239563820912)
XLA Ops:
  0.0 0.0 copy-start.2
  0.0 1.3 copy-done.2
  1.3 0.0 copy-start.7
  1.3 3.5 %turn.1 = f32[4624,128]{1,0:T(8,128)} custom-call(s32[32]{0:T(128)} %counts_in.1, f32[2592,128]{1,0:T(8,128)S(1)} %bitcast.4), custom_call_target="tpu_custom_call" | custom-call | tf_op jit(solution)/shard_map/turn/pallas_call | solution.py:455
  4.8 0.0 copy-done.7
  4.9 0.1 reshape.19
  4.9 0.1 reduce_sum.19
  5.1 0.6 reduce_max.19
  6.3 0.0 copy-start.8
  6.4 0.0 copy-start.1
  6.4 0.0 copy-start.3
  6.4 0.0 copy-start.4
  6.4 0.0 copy-start.6
  6.4 128.3 %conditional.2 = ((f32[8,152,384]{2,1,0:T(8,128)}, f32[8,144,384]{2,1,0:T(8,128)}, f32[8,144,384]{2,1,0:T(8,128)})) conditional(s32[]{:T(128)} %convert_element_type.7, (s32[32]{0:T(128)S(1)}, f32[4624,128]{1,0:T(8,128)}) %tuple.27, (s32[32]{0:T(128)S(1)}, f32[4624,128]{1,0:T(8,128)}) %tuple.28), branch_computations={%region_4.0_spmd, %region_5.0_spmd} | conditional | bytes 8 | solution.py:465
  6.4 128.3 %entry2.1 = (f32[8,152,384]{2,1,0:T(8,128)}, f32[8,144,384]{2,1,0:T(8,128)}, f32[8,144,384]{2,1,0:T(8,128)}) custom-call(s32[32]{0:T(128)S(1)} %get-tuple-element.26.counts, f32[4624,128]{1,0:T(8,128)} %get-tuple-element.27.turned), custom_call_target="tpu_custom_call" | custom-call | tf_op jit(solution)/shard_map/cond/branch_1_fun/entry2/pallas_call | solution.py:214
  134.7 0.0 copy-done.8
  134.7 0.0 copy-done.1
  134.7 0.0 copy-done.3
  134.7 0.0 copy-done.4
  134.7 0.0 copy-done.6
  134.8 8.0 %middle.1 = f32[8,144,384]{2,1,0:T(8,128)} custom-call(s32[32]{0:T(128)S(1)} %copy-done.7, s32[32]{0:T(128)S(1)} %copy-done.6, f32[11]{0:T(128)S(1)} %copy-done.4, f32[8,152,384]{2,1,0:T(8,128)} %get-tuple-element.35.own, f32[8,144,384]{2,1,0:T(8,128)} %get-tuple-element.36.cross, f32[8,144,384]{2,1,0:T(8,128)} %get-tuple-element.37.mate, ...), custom_call_target="tpu_custom_call" | custom-call | tf_op jit(solution)/shard_map/middle/pallas_call | solution.py:322
  142.8 0.1 reshape.18
  142.8 0.1 reduce_sum.18
  143.0 0.6 reduce_max.18
  144.3 0.0 copy-start
  144.3 0.0 copy-start.5
  144.3 109.6 %conditional.3 = (f32[4608,128]{1,0:T(8,128)}) conditional(s32[]{:T(128)} %convert_element_type.6, (s32[32]{0:T(128)S(1)}, f32[8,144,384]{2,1,0:T(8,128)}) %tuple.25, (s32[32]{0:T(128)S(1)}, f32[8,144,384]{2,1,0:T(8,128)}) %tuple.26), branch_computations={%region_6.0_spmd, %region_7.0_spmd} | conditional | bytes 8 | solution.py:476
  144.3 109.6 %leave3.1 = f32[4608,128]{1,0:T(8,128)} custom-call(s32[32]{0:T(128)S(1)} %get-tuple-element.28.counts, f32[8,144,384]{2,1,0:T(8,128)} %get-tuple-element.29.packed), custom_call_target="tpu_custom_call" | custom-call | tf_op jit(solution)/shard_map/cond/branch_0_fun/leave3/pallas_call | solution.py:403
  253.9 0.0 copy-done
  253.9 0.0 copy-done.5
  253.9 7.0 %last.1 = f32[2592,128]{1,0:T(8,128)} custom-call(s32[32]{0:T(128)S(1)} %copy-done.6, f32[35]{0:T(128)S(1)} %copy-done.5, f32[4608,128]{1,0:T(8,128)} %get-tuple-element.45.lines, f32[36,128,128]{2,1,0:T(8,128)S(1)} %copy-done), custom_call_target="tpu_custom_call" | custom-call | tf_op jit(solution)/shard_map/last/pallas_call | solution.py:483
  (1 shorter events, 0.0 us)
Async XLA Ops:
  0.0 1.3 copy-start.2
  1.3 3.5 %copy-start.7 = (s32[32]{0:T(128)S(1)}, s32[32]{0:T(128)}, u32[]{:S(2)}) copy-start(s32[32]{0:T(128)} %counts_in.1) | copy-start | bytes 388
  6.3 128.3 %copy-start.8 = (f32[1536]{0:T(1024)S(1)}, f32[1536]{0:T(1024)}, u32[]{:S(2)}) copy-start(f32[1536]{0:T(1024)} %param.15) | copy-start | bytes 18436
  6.4 128.4 %copy-start.1 = (bf16[3,1,144,1536]{3,2,1,0:T(8,128)(2,1)S(1)}, bf16[3,1,144,1536]{3,2,1,0:T(8,128)(2,1)}, u32[]{:S(2)}) copy-start(bf16[3,1,144,1536]{3,2,1,0:T(8,128)(2,1)} %param.14) | copy-start | bytes 3981316
  6.4 128.4 %copy-start.3 = (f32[12,128,128]{2,1,0:T(8,128)S(1)}, f32[12,128,128]{2,1,0:T(8,128)}, u32[]{:S(2)}) copy-start(f32[12,128,128]{2,1,0:T(8,128)} %inverse.2) | copy-start | bytes 2359300
  6.4 128.4 %copy-start.4 = (f32[11]{0:T(128)S(1)}, f32[11]{0:T(128)}, u32[]{:S(2)}) copy-start(f32[11]{0:T(128)} %link.2) | copy-start | bytes 136
  6.4 128.4 %copy-start.6 = (s32[32]{0:T(128)S(1)}, s32[32]{0:T(128)}, u32[]{:S(2)}) copy-start(s32[32]{0:T(128)} %counts.3) | copy-start | bytes 388
  144.3 109.6 %copy-start = (f32[36,128,128]{2,1,0:T(8,128)S(1)}, f32[36,128,128]{2,1,0:T(8,128)}, u32[]{:S(2)}) copy-start(f32[36,128,128]{2,1,0:T(8,128)} %inverse.3) | copy-start | bytes 7077892
  144.3 109.6 %copy-start.5 = (f32[35]{0:T(128)S(1)}, f32[35]{0:T(128)}, u32[]{:S(2)}) copy-start(f32[35]{0:T(128)} %link.3) | copy-start | bytes 424

commit v2 on v0

v2 whole, which is shorter than its diff:
```python
import functools
import jax
import jax.numpy as jnp
from jax import lax
from jax.experimental import pallas as pl
from jax.experimental.pallas import tpu as pltpu
from jax.sharding import PartitionSpec as P

MESH = pl.DeviceIdType.MESH
HIGH = lax.Precision.HIGH
B = 128
NQ = 8
QX = 4
ZL = 144
SLOTS = 72
KX = 12
KZ = 36
HALO = 8
NX = KX * B
CHUNKS = ((0, 48), (48, 48), (96, 48))
NC = len(CHUNKS)
F32 = jnp.float32
LIMIT = 48 * 2**20


def here():
    row = lax.axis_index("row")
    return row // QX, row % QX, lax.axis_index("col")


def starts_of(counts):
    starts, total = [], jnp.int32(0)
    for i in range(NQ * QX):
        starts.append(total)
        total = total + counts[i]
    return starts + [total]


def start_at(counts, row):
    total = jnp.int32(0)
    for i in range(NQ * QX - 1):
        total = total + jnp.where(i < row, counts[i], 0)
    return total


def turn_kernel(counts, temp, out):
    q, x, _ = here()
    shift = start_at(counts, QX * q + x) % B
    pad = jnp.zeros((B - SLOTS, B), F32)
    for k in range(KZ):
        block = temp[pl.ds(k, SLOTS, stride=KZ), :]
        turned = jnp.concatenate([block, pad], axis=0).T
        out[HALO + B * k : HALO + B * (k + 1), :] = pltpu.roll(turned, shift, 1)
    total = KZ * B
    out[0:HALO, :] = out[total : total + HALO, :]
    out[total + HALO : total + 2 * HALO, :] = out[HALO : 2 * HALO, :]


def across(c):
    return jnp.where(c % 2 == 1, (c + 1) % 16, (c + 15) % 16)


def barrier(partners):
    sem = pltpu.get_barrier_semaphore()
    for row, col in partners:
        pl.semaphore_signal(
            sem, inc=1, device_id={"row": row, "col": col}, device_id_type=MESH
        )
    pl.semaphore_wait(sem, len(partners))


def remote(src, dst, send, recv, row, col):
    return pltpu.make_async_remote_copy(
        src_ref=src,
        dst_ref=dst,
        send_sem=send,
        recv_sem=recv,
        device_id={"row": row, "col": col},
        device_id_type=MESH,
    )


ORDER = (7, 6, 5, 4, 3, 2, 1, 0)


def quad_tiles(q, most):
    low = max(QX * q, NX - most * (NQ - q))
    high = min(most * (q + 1), NX - QX * (NQ - 1 - q))
    return range(low // B, (high - 1) // B + 1)


def slot_masks(tiles, start, count, lane):
    first, shift = start // B, start % B
    masks = []
    for t in range(tiles):
        at_first = first % tiles == t
        at_second = (first + 1) % tiles == t
        low = jnp.where(at_first, shift, 2 * B)
        high = jnp.where(at_first, shift + count, 0)
        wrap = jnp.where(at_second, shift + count - B, 0)
        masks.append(((lane >= low) & (lane < high)) | (lane < wrap))
    return masks


def flow_kernel(
    tin, tout, counts_in, counts_out, link, turned, vel_hbm, spacing, inv_hbm, out,
    xin, merged, own, cross, mate, vel, inverse, field, edge, diff, right, solved, coef,
    packed, rz, piece,
    load, x_send, x_recv, x_local, o_send, o_recv, o_local, c_send, c_recv, m_send, m_recv,
    z_send, z_recv, y_send, y_recv, y_local,
):
    q, x, c = here()
    other, twin = across(c), c + 1 - 2 * (c % 2)
    row = QX * q + x
    loads = [
        pltpu.make_async_copy(vel_hbm, vel, load.at[0]),
        pltpu.make_async_copy(inv_hbm, inverse, load.at[1]),
    ]
    for cp in loads:
        cp.start()
    partners = [(QX * q + (x + s) % QX, c) for s in range(1, QX)]
    partners += [(QX * ((q + s) % NQ) + x, c) for s in range(1, NQ)]
    partners += [(QX * ((q + s) % NQ) + x, other) for s in range(NQ)]
    partners += [(row, twin)]
    barrier(partners)
    span = ZL + 2 * HALO

    def source(to_q, to_x):
        start = pl.multiple_of(QX * ZL * to_q + ZL * to_x, 8)
        return turned.at[pl.ds(start, span), :]

    x_copies = {}
    for s in ORDER:
        to_q = (q + s) % NQ
        local = pltpu.make_async_copy(source(to_q, x), xin.at[x, s], x_local.at[s])
        local.start()
        x_copies[s] = [local]
        for d in range(1, QX):
            to_x = (x + d) % QX
            cp = remote(
                source(to_q, to_x), xin.at[x, s], x_send.at[d, s], x_recv.at[d, s],
                QX * q + to_x, c,
            )
            cp.start()
            x_copies[s].append(cp)

    lane = lax.broadcasted_iota(jnp.int32, (8, B), 1)
    sub = lax.broadcasted_iota(jnp.int32, (8, B), 0)
    begin, takes = start_at(counts_in, QX * q), []
    for i in range(QX):
        count = counts_in[QX * q + i]
        takes.append(slot_masks(tin, begin, count, lane))
        begin = begin + count

    def send_rows(s, chunk):
        first, size = CHUNKS[chunk]
        to_q = (q + s) % NQ
        o_first = 0 if chunk == 0 else first + HALO
        o_size = size + HALO if chunk == 0 else size
        o_src, o_dst = merged.at[s, o_first : o_first + o_size], own.at[q, o_first : o_first + o_size]
        if s:
            o_copy = remote(
                o_src, o_dst, o_send.at[chunk, s], o_recv.at[chunk, s], QX * to_q + x, c
            )
        else:
            o_copy = pltpu.make_async_copy(o_src, o_dst, o_local.at[chunk])
        o_copy.start()
        c_copy = remote(
            merged.at[s, first + HALO : first + HALO + size], cross.at[q, first : first + size],
            c_send.at[chunk, s], c_recv.at[chunk, s], QX * to_q + x, other,
        )
        c_copy.start()
        return o_copy, c_copy

    o_copies, c_copies = {}, {}
    for s in ORDER:
        x_copies[s][0].wait()
        for cp in x_copies[s][1:]:
            cp.wait_recv()

        def put(to_row, parts):
            for t in range(tin):
                value = jnp.zeros((8, B), F32)
                for i in range(QX):
                    value = jnp.where(takes[i][t], parts[i], value)
                merged[s, pl.ds(to_row, 8), B * t : B * (t + 1)] = value

        def step(j, carry):
            r0 = pl.multiple_of(8 * j, 8) + HALO
            put(r0, [xin[i, s, pl.ds(r0, 8), :] for i in range(QX)])
            return carry

        lax.fori_loop(0, ZL // 8, step, 0)
        edges = []
        for i in range(QX):
            value = jnp.broadcast_to(xin[i, s, HALO - 1 : HALO, :], (8, B))
            rows = [ZL] + [first + size for first, size in CHUNKS[:-1]]
            for n, z in enumerate(rows):
                value = jnp.where(sub == 1 + n, xin[i, s, HALO + z : HALO + z + 1, :], value)
            edges.append(value)
        put(0, edges)
        o_copies[0, s], c_copies[0, s] = send_rows(s, 0)
    for chunk in range(1, NC):
        for s in ORDER:
            o_copies[chunk, s], c_copies[chunk, s] = send_rows(s, chunk)

    line = lax.broadcasted_iota(jnp.int32, (1, B), 1)
    begins_in = starts_of(counts_in)[::QX]
    begins_out = starts_of(counts_out)[::QX]
    sign = jnp.where(c % 2 == 0, F32(1), F32(-1))

    def covers(begins, p, t):
        return (line >= begins[p] - B * t) & (line < begins[p + 1] - B * t)

    def assemble(dst, to, size, read):
        for t in range(KX):
            value = jnp.zeros((size, B), F32)
            for p in range(NQ):
                if t in quad_tiles(p, most_in):
                    value = jnp.where(covers(begins_in, p, t), read(p, t % tin), value)
            dst[to : to + size, B * t : B * (t + 1)] = value

    most_in, most_out = QX * SLOTS, QX * SLOTS
    at = lax.broadcasted_iota(jnp.int32, (16, NX), 1)
    z_copies, m_copies = {}, {}
    for chunk, (first, size) in enumerate(CHUNKS):
        for s in range(NQ):
            from_q = (q + NQ - s) % NQ
            if s:
                o_copies[chunk, s].wait_recv()
            else:
                o_copies[chunk, s].wait()
            cp = remote(
                own.at[from_q, first + HALO : first + HALO + size],
                mate.at[from_q, first : first + size],
                m_send.at[chunk, s], m_recv.at[chunk, s], row, twin,
            )
            cp.start()
            m_copies[chunk, s] = cp
        if chunk == 0:
            assemble(edge, 0, HALO, lambda p, t: own[p, 0:HALO, B * t : B * (t + 1)])
            field[HALO - 1 : HALO, :] = edge[0:1, :]
        rows = slice(first, first + size)
        o_rows = slice(first + HALO, first + HALO + size)
        assemble(field, first + HALO, size, lambda p, t: own[p, o_rows, B * t : B * (t + 1)])
        last = 1 if chunk == NC - 1 else 2 + chunk
        after = first + HALO + size
        field[after : after + 1, :] = edge[last : last + 1, :]
        if chunk == 0:
            for cp in loads:
                cp.wait()
        for s in range(NQ):
            c_copies[chunk, s].wait_recv()
            m_copies[chunk, s].wait_recv()
        assemble(
            diff, first, size,
            lambda p, t: (
                mate[p, rows, B * t : B * (t + 1)] - cross[p, rows, B * t : B * (t + 1)]
            ) * sign,
        )
        for r in range(first, first + size, 16):
            r0 = r + HALO
            here_f = field[r0 : r0 + 16, :]
            low = jnp.where(at == 0, 0.0, pltpu.roll(here_f, 1, 1))
            high = jnp.where(at == NX - 1, 0.0, pltpu.roll(here_f, NX - 1, 1))
            grad_z = field[r0 + 1 : r0 + 17, :] - field[r0 - 1 : r0 + 15, :]
            u, v, w = [vel[j, r : r + 16, :].astype(F32) for j in range(3)]
            advection = u * ((high - low) * spacing[...])
            advection += 0.5 * (v * diff[r : r + 16, :]) + 0.5 * (w * grad_z)
            right[r : r + 16, :] = here_f - advection
        end = None
        for k in range(KX):
            across_k = inverse[k].T
            y = jnp.dot(
                right[rows, B * k : B * (k + 1)], across_k, precision=HIGH,
                preferred_element_type=F32,
            )
            if k:
                y = y + (link[k - 1] * across_k[0:1, :]) * end
            if k < KX - 1:
                coef[k : k + 1, :] = link[k] * across_k[B - 1 : B, :]
            end = y[:, B - 1 : B]
            solved[rows, B * k : B * (k + 1)] = y
        head = None
        for k in reversed(range(KX)):
            y = solved[rows, B * k : B * (k + 1)]
            if k < KX - 1:
                y = y + coef[k : k + 1, :] * head
                solved[rows, B * k : B * (k + 1)] = y
            head = y[:, 0:1]
        for p in range(NQ):
            for b in range(tout):
                value = jnp.zeros((size, B), F32)
                for t in quad_tiles(p, most_out):
                    if t % tout == b:
                        value = jnp.where(
                            covers(begins_out, p, t), solved[rows, B * t : B * (t + 1)], value
                        )
                packed[p, rows, B * b : B * (b + 1)] = value
        for s in range(NQ - 1, 0, -1):
            to_q = (q + s) % NQ
            cp = remote(
                packed.at[to_q, rows], rz.at[q, rows],
                z_send.at[chunk, s], z_recv.at[chunk, s], QX * to_q + x, c,
            )
            cp.start()
            z_copies[chunk, s] = cp

    pieces = []
    for i in range(QX):
        at_row = QX * q + (x + i) % QX
        pieces.append(slot_masks(tout, start_at(counts_out, at_row), counts_out[at_row], lane))
    y_copies = []
    for chunk, (first, size) in enumerate(CHUNKS):
        for s in range(NQ):
            from_q = (q + NQ - s) % NQ
            if s:
                z_copies[chunk, s].wait_recv()

            def step(j, carry):
                at_rows = pl.ds(pl.multiple_of(first + 8 * j, 8), 8)
                if s:
                    parts = [rz[from_q, at_rows, B * t : B * (t + 1)] for t in range(tout)]
                else:
                    parts = [packed[q, at_rows, B * t : B * (t + 1)] for t in range(tout)]
                for d in range(QX):
                    value = jnp.zeros((8, B), F32)
                    for t in range(tout):
                        value = jnp.where(pieces[d][t], parts[t], value)
                    piece[d, s, at_rows, :] = value
                return carry

            lax.fori_loop(0, size // 8, step, 0)
            to = pl.multiple_of(ZL * (QX * from_q + x) + first, 8)
            for d in range(QX):
                part, goal = piece.at[d, s, first : first + size], out.at[pl.ds(to, size), :]
                if d:
                    cp = remote(
                        part, goal, y_send.at[chunk, d, s], y_recv.at[chunk, d, s],
                        QX * q + (x + d) % QX, c,
                    )
                else:
                    cp = pltpu.make_async_copy(part, goal, y_local.at[chunk, s])
                cp.start()
                y_copies.append(cp)
    for cp in y_copies:
        cp.wait()
    for chunk in range(NC):
        for s in range(NQ):
            m_copies[chunk, s].wait_send()
            c_copies[chunk, s].wait_send()
            if s:
                o_copies[chunk, s].wait_send()
                z_copies[chunk, s].wait_send()
    for s in range(NQ):
        for cp in x_copies[s][1:]:
            cp.wait_send()


def flow(tin, tout, cid, counts_in, counts_out, link, turned, vel, spacing, inverse):
    dma = pltpu.SemaphoreType.DMA
    vmem = pl.BlockSpec(memory_space=pltpu.VMEM)
    smem = pl.BlockSpec(memory_space=pltpu.SMEM)
    hbm = pl.BlockSpec(memory_space=pl.ANY)
    rows = ZL + HALO
    per = dma((NC, NQ))
    return pl.pallas_call(
        functools.partial(flow_kernel, tin, tout),
        name="flow%d%d" % (tin, tout),
        out_shape=jax.ShapeDtypeStruct((KZ * B, B), F32),
        in_specs=[smem, smem, smem, vmem, hbm, vmem, hbm],
        out_specs=hbm,
        scratch_shapes=[
            pltpu.VMEM((QX, NQ, ZL + 2 * HALO, B), F32),
            pltpu.VMEM((NQ, rows, tin * B), F32),
            pltpu.VMEM((NQ, rows, tin * B), F32),
            pltpu.VMEM((NQ, ZL, tin * B), F32),
            pltpu.VMEM((NQ, ZL, tin * B), F32),
            pltpu.VMEM((3, ZL, NX), jnp.bfloat16),
            pltpu.VMEM((KX, B, B), F32),
            pltpu.VMEM((ZL + 2 * HALO, NX), F32),
            pltpu.VMEM((HALO, NX), F32),
            pltpu.VMEM((ZL, NX), F32),
            pltpu.VMEM((ZL, NX), F32),
            pltpu.VMEM((ZL, NX), F32),
            pltpu.VMEM((KX + 4, B), F32),
            pltpu.VMEM((NQ, ZL, tout * B), F32),
            pltpu.VMEM((NQ, ZL, tout * B), F32),
            pltpu.VMEM((QX, NQ, ZL, B), F32),
            dma((2,)), dma((QX, NQ)), dma((QX, NQ)), dma((NQ,)),
            per, per, dma((NC,)), per, per, per, per, per, per,
            dma((NC, QX, NQ)), dma((NC, QX, NQ)), per,
        ],
        compiler_params=pltpu.CompilerParams(
            collective_id=cid, has_side_effects=True, vmem_limit_bytes=LIMIT
        ),
    )(counts_in, counts_out, link, turned, vel, spacing, inverse)


def last_kernel(counts, link, lines, inverse, out, solved):
    q, x, _ = here()
    back = (B - start_at(counts, QX * q + x) % B) % B
    count = counts[QX * q + x]
    valid = lax.broadcasted_iota(jnp.int32, (SLOTS, B), 0) < count
    end = None
    for k in range(KZ):
        y = jnp.dot(
            inverse[k], lines[B * k : B * (k + 1), :], precision=HIGH,
            preferred_element_type=F32,
        )
        if k:
            y = y + (link[k - 1] * inverse[k, :, 0:1]) * end
        end = y[B - 1 : B, :]
        solved[B * k : B * (k + 1), :] = y
    head = None
    for k in reversed(range(KZ)):
        y = solved[B * k : B * (k + 1), :]
        if k < KZ - 1:
            y = y + (link[k] * inverse[k, :, B - 1 : B]) * head
        head = y[0:1, :]
        turned = pltpu.roll(y, back, 1).T
        out[pl.ds(k, SLOTS, stride=KZ), :] = jnp.where(valid, turned[0:SLOTS, :], 0.0)


def on_device(
    temp_in, velocity, spacing_x, inverse_x, link_x, inverse_z, link_z, counts_in, counts_out
):
    vmem = pl.BlockSpec(memory_space=pltpu.VMEM)
    smem = pl.BlockSpec(memory_space=pltpu.SMEM)
    local = pltpu.CompilerParams(vmem_limit_bytes=LIMIT)
    turned = pl.pallas_call(
        turn_kernel,
        name="turn",
        out_shape=jax.ShapeDtypeStruct((KZ * B + 2 * HALO, B), F32),
        in_specs=[smem, vmem],
        out_specs=vmem,
        compiler_params=local,
    )(counts_in, temp_in.reshape(SLOTS * KZ, B))
    sums = jnp.sum(jnp.stack([counts_in, counts_out]).reshape(2, NQ, QX), axis=2)
    wide = (jnp.max(sums, axis=1) > 2 * B).astype(jnp.int32)
    lines = lax.switch(
        2 * wide[0] + wide[1],
        [
            functools.partial(flow, tin, tout, 1 + i)
            for i, (tin, tout) in enumerate(((2, 2), (2, 3), (3, 2), (3, 3)))
        ],
        counts_in, counts_out, link_x, turned,
        velocity.reshape(3, ZL, NX), spacing_x.reshape(1, NX), inverse_x,
    )
    out = pl.pallas_call(
        last_kernel,
        name="last",
        out_shape=jax.ShapeDtypeStruct((SLOTS * KZ, B), F32),
        in_specs=[smem, smem, vmem, vmem],
        out_specs=vmem,
        scratch_shapes=[pltpu.VMEM((KZ * B, B), F32)],
        compiler_params=local,
    )(counts_out, link_z, lines, inverse_z)
    return out.reshape(SLOTS, 1, KZ * B)


def solution(mesh):
    in_specs = (
        P("row", "col", None),
        P(None, "col", "row", None),
        P(),
        P(),
        P(),
        P(),
        P(),
        P(),
        P(),
    )
    out_specs = P("row", "col", None)
    return jax.shard_map(
        on_device, mesh=mesh, in_specs=in_specs, out_specs=out_specs, check_vma=False
    )
```

time: 450 us -> 238 us (0.53)
  waiting for transfers between devices: 243 us -> 0 us
  Pallas kernels: 0 us -> 229 us
  local copies, waits for them, and re-layouts: 95 us -> 4.18 us
  starting transfers between devices: 75.8 us -> 0 us
  other arithmetic: 25.3 us -> 0.27 us
  matrix products: 9.02 us -> 0 us
    pallas_call x0 -> x3, Pallas kernels: none -> 229 us  [the longest x1 219 us: flow(): pl.pallas_call(functools.partial(flow_kernel, tin, tout), name='flow%d%d'...]
    all_to_all x2 -> x0, waiting for transfers between devices: 197 us -> none  [the longest x1 104 us: on_device(): lax.all_to_all(temp_in, 'row', split_axis=2, concat_axis=0, tiled=True)]
    all_to_all x2 -> x0, starting transfers between devices: 47.4 us -> none  [the longest x1 31.3 us: on_device(): lax.all_to_all(outgoing, 'row', split_axis=2, concat_axis=1, tiled=True)]
    ppermute x4 -> x0, waiting for transfers between devices: 46 us -> none  [the longest x2 46 us: padded_2(): lax.ppermute(lax.slice_in_dim(block, 0, width, axis=dim), axis, backward)]
    ppermute x4 -> x0, starting transfers between devices: 28.4 us -> none  [the longest x2 15.5 us: padded_2(): lax.ppermute(lax.slice_in_dim(block, 0, width, axis=dim), axis, backward)]
    unnamed x40 -> x16, local copies, waits for them, and re-layouts: 26.9 us -> 1.35 us
    slice x59 -> x1, local copies, waits for them, and re-layouts: 20.2 us -> 0.59 us  [on_device(): wide[1]]
    all_to_all x4 -> x0, local copies, waits for them, and re-layouts: 13.4 us -> none  [the longest x2 7.4 us: on_device(): lax.all_to_all(outgoing, 'row', split_axis=2, concat_axis=1, tiled=True)]
  transfers between devices with their start and end apart: 6 -> 0, of which waited for: 3 -> 0; matrix products, arithmetic and copies ran while one was open for 7% -> 0% of each run, Pallas kernels for 0% -> 0%
where the time goes in v2:
time: 238 us; the launch traced here: 235 us
  Pallas kernels  229 us (96%)
  local copies, waits for them, and re-layouts  4.18 us (2%)
    pallas_call x1, Pallas kernels, flow(): pl.pallas_call(functools.partial(flow_kernel, tin, tout), name='flow%d%d'...  219 us
    pallas_call x1, Pallas kernels, on_device(): pl.pallas_call(last_kernel, name='last', out_shape=jax.ShapeDtypeStruct((...  7 us

profile of v2, /device:TPU:1, one launch (start us, length us, event | category | flops | bytes accessed | tf_op | source)
XLA Modules:
  0.0 235.2 jit_solution(14243365379330128236)
XLA Ops:
  0.0 0.0 copy-start.5
  0.0 0.0 copy-start.6
  0.0 0.0 copy-start.7
  0.0 0.8 stack.9
  0.8 0.7 stack.10
  1.5 0.1 add_reduce_fusion
  1.7 0.1 reduce_max.9
  1.8 0.6 fusion
  3.8 0.7 reshape.25
  4.5 0.0 copy-start.1
  4.5 1.3 copy-done.1
  5.8 0.0 copy-start.3
  5.8 0.0 copy-start.4
  5.8 2.1 turn.1
  7.9 0.0 copy-done.5
  7.9 0.0 copy-done.6
  7.9 0.0 copy-done.7
  7.9 0.0 copy-done.3
  7.9 0.0 copy-done.4
  7.9 0.0 copy-start
  7.9 0.0 copy-start.2
  8.0 220.2 %conditional.1 = (f32[4608,128]{1,0:T(8,128)}) conditional(s32[]{:T(128)} %bitcast, (s32[32]{0:T(128)S(1)}, s32[32]{0:T(128)S(1)}, f32[11]{0:T(128)S(1)}, f32[4624,128]{1,0:T(8,128)S(1)}, bf16[3,144,1536]{2,1,0:T(8,128)(2,1)S(1)}, /*index=5*/f32[1,1536]{1,0:T(1,128)S(1)}, f32[12,128,128]{2,1,0:T(8,128)S(1)}) %tuple.39, ...), branch_computations={%region_2.0_spmd, %region_3.0_spmd, %region_4.0_spmd, %region_5.0_... | conditional | bytes 8 | solution.py:441
  8.2 219.4 %flow23.1 = f32[4608,128]{1,0:T(8,128)} custom-call(s32[32]{0:T(128)S(1)} %get-tuple-element.73.counts_in, s32[32]{0:T(128)S(1)} %get-tuple-element.74.counts_out, f32[11]{0:T(128)S(1)} %get-tuple-element.75.link, f32[4624,128]{1,0:T(8,128)S(1)} %get-tuple-element.76.turned, bf16[3,144,1536]{2,1,0:T(8,128)(2,1)S(1)} %get-tuple-element.77.vel_hbm, ...), custom_call_target="tpu_custom_call" | custom-call | tf_op jit(solution)/shard_map/cond/branch_1_fun/flow23/pallas_call | solution.py:367
  228.1 0.0 copy-done
  228.1 0.0 copy-done.2
  228.2 7.0 %last.1 = f32[2592,128]{1,0:T(8,128)} custom-call(s32[32]{0:T(128)S(1)} %copy-done.5, f32[35]{0:T(128)S(1)} %copy-done.2, f32[4608,128]{1,0:T(8,128)} %get-tuple-element.96.lines, f32[36,128,128]{2,1,0:T(8,128)S(1)} %copy-done), custom_call_target="tpu_custom_call" | custom-call | tf_op jit(solution)/shard_map/last/pallas_call | solution.py:450
  (1 shorter events, 0.0 us)
Async XLA Ops:
  0.0 7.9 %copy-start.5 = (s32[32]{0:T(128)S(1)}, s32[32]{0:T(128)}, u32[]{:S(2)}) copy-start(s32[32]{0:T(128)} %counts.3) | copy-start | bytes 388
  0.0 7.9 %copy-start.6 = (s32[32]{0:T(128)S(1)}, s32[32]{0:T(128)}, u32[]{:S(2)}) copy-start(s32[32]{0:T(128)} %counts.2) | copy-start | bytes 388
  0.0 7.9 %copy-start.7 = (f32[11]{0:T(128)S(1)}, f32[11]{0:T(128)}, u32[]{:S(2)}) copy-start(f32[11]{0:T(128)} %param.17) | copy-start | bytes 136
  4.5 1.3 copy-start.1
  5.8 2.1 copy-start.3
  5.8 2.1 copy-start.4
  7.9 220.2 %copy-start = (f32[36,128,128]{2,1,0:T(8,128)S(1)}, f32[36,128,128]{2,1,0:T(8,128)}, u32[]{:S(2)}) copy-start(f32[36,128,128]{2,1,0:T(8,128)} %inverse.1) | copy-start | bytes 7077892
  7.9 220.2 %copy-start.2 = (f32[35]{0:T(128)S(1)}, f32[35]{0:T(128)}, u32[]{:S(2)}) copy-start(f32[35]{0:T(128)} %link.1) | copy-start | bytes 424

commit v3 on v2

--- a/solution.py
+++ b/solution.py
@@ -16,6 +16,10 @@
 KX = 12
 KZ = 36
 HALO = 8
+QUAD = 192
+SPAN = ZL + 2 * HALO
+RING = 256
+REST = 16
 NX = KX * B
 CHUNKS = ((0, 48), (48, 48), (96, 48))
 NC = len(CHUNKS)
@@ -43,9 +47,16 @@
     return total
 
 
-def turn_kernel(counts, temp, out):
+def turn_kernel(counts_in, counts_out, temp, out, pick):
     q, x, _ = here()
-    shift = start_at(counts, QX * q + x) % B
+    shift = start_at(counts_in, QX * q + x) % B
+    starts = starts_of(counts_in)
+    drift, most = jnp.int32(0), jnp.int32(0)
+    ends = starts_of(counts_out)
+    for p in range(NQ):
+        drift = jnp.maximum(drift, jnp.abs(starts[QX * p] - QUAD * p))
+        most = jnp.maximum(most, ends[QX * (p + 1)] - ends[QX * p])
+    pick[0] = jnp.where(drift > B, 2, jnp.where(most > RING, 1, 0))
     pad = jnp.zeros((B - SLOTS, B), F32)
     for k in range(KZ):
         block = temp[pl.ds(k, SLOTS, stride=KZ), :]
@@ -80,7 +91,8 @@
     )
 
 
-ORDER = (7, 6, 5, 4, 3, 2, 1, 0)
+ORDER = (4, 3, 5, 2, 6, 1, 7, 0)
+LAG = 2
 
 
 def quad_tiles(q, most):
@@ -102,13 +114,37 @@
     return masks
 
 
+class Layout:
+    def __init__(self, per_row, halo):
+        self.halo = halo
+        self.rows = [size * per_row // 2 for _, size in CHUNKS]
+        self.at = [sum(self.rows[:i]) for i in range(NC)]
+        self.total = sum(self.rows)
+
+    def own(self, chunk):
+        if chunk == 0:
+            return pl.ds(0, self.halo + self.rows[0])
+        return pl.ds(self.halo + self.at[chunk], self.rows[chunk])
+
+    def inner(self, chunk):
+        return pl.ds(self.halo + self.at[chunk], self.rows[chunk])
+
+    def bare(self, chunk):
+        return pl.ds(self.at[chunk], self.rows[chunk])
+
+
+EVEN = Layout(3, HALO)
+WIDE = Layout(6, 3 * HALO)
+
+
 def flow_kernel(
-    tin, tout, counts_in, counts_out, link, turned, vel_hbm, spacing, inv_hbm, out,
-    xin, merged, own, cross, mate, vel, inverse, field, edge, diff, right, solved, coef,
-    packed, rz, piece,
+    even, wide_out, counts_in, counts_out, link, turned, vel_hbm, spacing, inv_hbm, out,
+    xin, merged, own, cross, mate, away, come, vel, inverse, field, edge, diff, right, solved,
+    coef, scale, packed, rz, piece,
     load, x_send, x_recv, x_local, o_send, o_recv, o_local, c_send, c_recv, m_send, m_recv,
-    z_send, z_recv, y_send, y_recv, y_local,
+    n_send, n_recv, z_send, z_recv, y_send, y_recv, y_local,
 ):
+    lay = EVEN if even else WIDE
     q, x, c = here()
     other, twin = across(c), c + 1 - 2 * (c % 2)
     row = QX * q + x
@@ -123,11 +159,10 @@
     partners += [(QX * ((q + s) % NQ) + x, other) for s in range(NQ)]
     partners += [(row, twin)]
     barrier(partners)
-    span = ZL + 2 * HALO
 
     def source(to_q, to_x):
         start = pl.multiple_of(QX * ZL * to_q + ZL * to_x, 8)
-        return turned.at[pl.ds(start, span), :]
+        return turned.at[pl.ds(start, SPAN), :]
 
     x_copies = {}
     for s in ORDER:
@@ -146,18 +181,142 @@
 
     lane = lax.broadcasted_iota(jnp.int32, (8, B), 1)
     sub = lax.broadcasted_iota(jnp.int32, (8, B), 0)
-    begin, takes = start_at(counts_in, QX * q), []
+    edge_rows = [-1, ZL] + [first + size for first, size in CHUNKS[:-1]]
+    quad_first = start_at(counts_in, QX * q)
+    firsts = [quad_first]
     for i in range(QX):
-        count = counts_in[QX * q + i]
-        takes.append(slot_masks(tin, begin, count, lane))
-        begin = begin + count
+        firsts.append(firsts[-1] + counts_in[QX * q + i])
+
+    def choose(masks, parts):
+        value = jnp.zeros((8, B), F32)
+        for mask, part in zip(masks, parts):
+            value = jnp.where(mask, part, value)
+        return value
+
+    def arrived(s):
+        x_copies[s][0].wait()
+        for cp in x_copies[s][1:]:
+            cp.wait_recv()
+
+    def edge_parts(s, rows, read):
+        value = jnp.zeros((8, B), F32)
+        for n, z in rows:
+            value = jnp.where(sub == n, read(z), value)
+        return value
+
+    n_copies = {}
+    if even:
+        odd = q % 2
+        full_at = QUAD * q + (B // 2) * odd
+        half_at = QUAD * q + B - (3 * B // 2) * odd
+        natural = (lane < B // 2) == (jnp.zeros((8, B), jnp.int32) + odd == 0)
+
+        def inside(place):
+            return [(place >= firsts[i]) & (place < firsts[i + 1]) for i in range(QX)]
+
+        def quad_masks(place):
+            return inside(place) + [place < firsts[0], place >= firsts[QX]]
+
+        full_masks, half_masks = quad_masks(lane + full_at), quad_masks(lane + half_at)
+        window_masks = []
+        for base in (QUAD * (q + 1), QUAD * q - B):
+            turn = (base + B) % B
+            window_masks.append(inside(lane + (base - turn) + jnp.where(lane < turn, B, 0)))
+
+        def prepare(s):
+            arrived(s)
+
+            def step(j, carry):
+                rows = pl.ds(pl.multiple_of(8 * j, 8), 8)
+                parts = [xin[i, s, rows, :] for i in range(QX)]
+                for side in range(2):
+                    away[side, s, rows, :] = choose(window_masks[side], parts)
+                return carry
+
+            lax.fori_loop(0, SPAN // 8, step, 0)
+            to_q = (q + s) % NQ
+            for side, (inner, to) in enumerate(((q < NQ - 1, q + 1), (q > 0, q - 1))):
+                to = (to + NQ) % NQ
+                cp = remote(
+                    away.at[side, s], come.at[side, to_q],
+                    n_send.at[side, to_q], n_recv.at[side, to_q], QX * to + x, c,
+                )
+                n_copies[side, s] = cp
+                pl.when(inner)(cp.start)
+
+        def merge(s):
+            to_q = (q + s) % NQ
+            pl.when(q > 0)(n_copies[0, s].wait_recv)
+            pl.when(q < NQ - 1)(n_copies[1, s].wait_recv)
+
+            def parts_at(rows):
+                parts = [xin[i, s, rows, :] for i in range(QX)]
+                return parts + [come[side, to_q, rows, :] for side in range(2)]
+
+            for chunk, (first, size) in enumerate(CHUNKS):
+                base = lay.halo + lay.at[chunk]
+
+                def step(j, carry):
+                    r = pl.multiple_of(8 * j, 8)
+                    halves = []
+                    for up in (0, size // 2):
+                        parts = parts_at(pl.ds(HALO + first + up + r, 8))
+                        merged[s, pl.ds(base + up + r, 8), :] = choose(full_masks, parts)
+                        halves.append(choose(half_masks, parts))
+                    merged[s, pl.ds(base + size + r, 8), :] = jnp.where(
+                        natural, halves[0], pltpu.roll(halves[1], B // 2, 1)
+                    )
+                    return carry
+
+                lax.fori_loop(0, size // 16, step, 0)
+            parts = []
+            for rows in (
+                [lambda z, i=i: xin[i, s, HALO + z : HALO + z + 1, :] for i in range(QX)]
+                + [lambda z, i=i: come[i, to_q, HALO + z : HALO + z + 1, :] for i in range(2)]
+            ):
+                pairs = [(n, z) for n, z in enumerate(edge_rows)]
+                parts.append(edge_parts(s, pairs + [(4 + n, z) for n, z in pairs], rows))
+            merged[s, 0:HALO, :] = jnp.where(
+                sub < 4, choose(full_masks, parts), choose(half_masks, parts)
+            )
+
+    else:
+        takes = [
+            slot_masks(3, firsts[i], firsts[i + 1] - firsts[i], lane) for i in range(QX)
+        ]
+
+        def prepare(s):
+            arrived(s)
+
+        def merge(s):
+            for chunk, (first, size) in enumerate(CHUNKS):
+                base = lay.halo + lay.at[chunk]
+
+                def step(j, carry):
+                    r = pl.multiple_of(8 * j, 8)
+                    parts = [xin[i, s, pl.ds(HALO + first + r, 8), :] for i in range(QX)]
+                    for t in range(3):
+                        merged[s, pl.ds(base + t * size + r, 8), :] = choose(
+                            [takes[i][t] for i in range(QX)], parts
+                        )
+                    return carry
+
+                lax.fori_loop(0, size // 8, step, 0)
+            parts = [
+                edge_parts(
+                    s, list(enumerate(edge_rows)),
+                    lambda z, i=i: xin[i, s, HALO + z : HALO + z + 1, :],
+                )
+                for i in range(QX)
+            ]
+            for t in range(3):
+                merged[s, HALO * t : HALO * (t + 1), :] = choose(
+                    [takes[i][t] for i in range(QX)], parts
+                )
 
     def send_rows(s, chunk):
-        first, size = CHUNKS[chunk]
         to_q = (q + s) % NQ
-        o_first = 0 if chunk == 0 else first + HALO
-        o_size = size + HALO if chunk == 0 else size
-        o_src, o_dst = merged.at[s, o_first : o_first + o_size], own.at[q, o_first : o_first + o_size]
+        o_src, o_dst = merged.at[s, lay.own(chunk)], own.at[q, lay.own(chunk)]
         if s:
             o_copy = remote(
                 o_src, o_dst, o_send.at[chunk, s], o_recv.at[chunk, s], QX * to_q + x, c
@@ -166,40 +325,21 @@
             o_copy = pltpu.make_async_copy(o_src, o_dst, o_local.at[chunk])
         o_copy.start()
         c_copy = remote(
-            merged.at[s, first + HALO : first + HALO + size], cross.at[q, first : first + size],
+            merged.at[s, lay.inner(chunk)], cross.at[q, lay.bare(chunk)],
             c_send.at[chunk, s], c_recv.at[chunk, s], QX * to_q + x, other,
         )
         c_copy.start()
         return o_copy, c_copy
 
     o_copies, c_copies = {}, {}
-    for s in ORDER:
-        x_copies[s][0].wait()
-        for cp in x_copies[s][1:]:
-            cp.wait_recv()
-
-        def put(to_row, parts):
-            for t in range(tin):
-                value = jnp.zeros((8, B), F32)
-                for i in range(QX):
-                    value = jnp.where(takes[i][t], parts[i], value)
-                merged[s, pl.ds(to_row, 8), B * t : B * (t + 1)] = value
-
-        def step(j, carry):
-            r0 = pl.multiple_of(8 * j, 8) + HALO
-            put(r0, [xin[i, s, pl.ds(r0, 8), :] for i in range(QX)])
-            return carry
-
-        lax.fori_loop(0, ZL // 8, step, 0)
-        edges = []
-        for i in range(QX):
-            value = jnp.broadcast_to(xin[i, s, HALO - 1 : HALO, :], (8, B))
-            rows = [ZL] + [first + size for first, size in CHUNKS[:-1]]
-            for n, z in enumerate(rows):
-                value = jnp.where(sub == 1 + n, xin[i, s, HALO + z : HALO + z + 1, :], value)
-            edges.append(value)
-        put(0, edges)
-        o_copies[0, s], c_copies[0, s] = send_rows(s, 0)
+    lag = LAG if even else 0
+    for n in range(NQ + lag):
+        if n < NQ:
+            prepare(ORDER[n])
+        if n >= lag:
+            s = ORDER[n - lag]
+            merge(s)
+            o_copies[0, s], c_copies[0, s] = send_rows(s, 0)
     for chunk in range(1, NC):
         for s in ORDER:
             o_copies[chunk, s], c_copies[chunk, s] = send_rows(s, chunk)
@@ -208,20 +348,50 @@
     begins_in = starts_of(counts_in)[::QX]
     begins_out = starts_of(counts_out)[::QX]
     sign = jnp.where(c % 2 == 0, F32(1), F32(-1))
-
-    def covers(begins, p, t):
-        return (line >= begins[p] - B * t) & (line < begins[p + 1] - B * t)
+    most = QX * SLOTS
+
+    def covers(low, high, t):
+        return (line >= low - B * t) & (line < high - B * t)
 
     def assemble(dst, to, size, read):
-        for t in range(KX):
-            value = jnp.zeros((size, B), F32)
-            for p in range(NQ):
-                if t in quad_tiles(p, most_in):
-                    value = jnp.where(covers(begins_in, p, t), read(p, t % tin), value)
-            dst[to : to + size, B * t : B * (t + 1)] = value
-
-    most_in, most_out = QX * SLOTS, QX * SLOTS
+        if not even:
+            for t in range(KX):
+                value = jnp.zeros((size, B), F32)
+                for p in range(NQ):
+                    if t in quad_tiles(p, most):
+                        mask = covers(begins_in[p], begins_in[p + 1], t)
+                        value = jnp.where(mask, read(p, size * (t % 3), size), value)
+                dst[to : to + size, B * t : B * (t + 1)] = value
+            return
+        h = size // 2
+        for m in range(NQ // 2):
+            lo, hi = 2 * m, 2 * m + 1
+            cols = [slice(B * (3 * m + t), B * (3 * m + t + 1)) for t in range(3)]
+            dst[to : to + size, cols[0]] = read(lo, 0, size)
+            dst[to : to + size, cols[2]] = read(hi, 0, size)
+            a, b = read(lo, size, h), read(hi, size, h)
+            dst[to : to + h, cols[1]] = jnp.where(line < B // 2, a, b)
+            dst[to + h : to + size, cols[1]] = pltpu.roll(
+                jnp.where(line < B // 2, b, a), B // 2, 1
+            )
+
+    def assemble_edge():
+        if not even:
+            assemble(edge, 0, HALO, lambda p, r, n: own[p, r : r + n, :])
+            return
+        for m in range(NQ // 2):
+            lo, hi = own[2 * m, 0:HALO, :], own[2 * m + 1, 0:HALO, :]
+            at = 3 * m * B
+            edge[0:4, at : at + B] = lo[0:4]
+            edge[0:4, at + B : at + 2 * B] = jnp.where(line < B // 2, lo, hi)[4:8]
+            edge[0:4, at + 2 * B : at + 3 * B] = hi[0:4]
+
+    for t in range(KX):
+        scale[0:1, B * t : B * (t + 1)] = spacing[t : t + 1, :]
     at = lax.broadcasted_iota(jnp.int32, (16, NX), 1)
+    per_out = 2 * 48 + (REST if wide_out else 0)
+    group = lane // 32
+    group16 = lax.broadcasted_iota(jnp.int32, (REST, B), 1) // 32
     z_copies, m_copies = {}, {}
     for chunk, (first, size) in enumerate(CHUNKS):
         for s in range(NQ):
@@ -231,18 +401,19 @@
             else:
                 o_copies[chunk, s].wait()
             cp = remote(
-                own.at[from_q, first + HALO : first + HALO + size],
-                mate.at[from_q, first : first + size],
+                own.at[from_q, lay.inner(chunk)], mate.at[from_q, lay.bare(chunk)],
                 m_send.at[chunk, s], m_recv.at[chunk, s], row, twin,
             )
             cp.start()
             m_copies[chunk, s] = cp
         if chunk == 0:
-            assemble(edge, 0, HALO, lambda p, t: own[p, 0:HALO, B * t : B * (t + 1)])
+            assemble_edge()
             field[HALO - 1 : HALO, :] = edge[0:1, :]
         rows = slice(first, first + size)
-        o_rows = slice(first + HALO, first + HALO + size)
-        assemble(field, first + HALO, size, lambda p, t: own[p, o_rows, B * t : B * (t + 1)])
+        o_at, c_at = lay.halo + lay.at[chunk], lay.at[chunk]
+        assemble(
+            field, first + HALO, size, lambda p, r, n: own[p, o_at + r : o_at + r + n, :]
+        )
         last = 1 if chunk == NC - 1 else 2 + chunk
         after = first + HALO + size
         field[after : after + 1, :] = edge[last : last + 1, :]
@@ -254,8 +425,8 @@
             m_copies[chunk, s].wait_recv()
         assemble(
             diff, first, size,
-            lambda p, t: (
-                mate[p, rows, B * t : B * (t + 1)] - cross[p, rows, B * t : B * (t + 1)]
+            lambda p, r, n: (
+                mate[p, c_at + r : c_at + r + n, :] - cross[p, c_at + r : c_at + r + n, :]
             ) * sign,
         )
         for r in range(first, first + size, 16):
@@ -265,7 +436,7 @@
             high = jnp.where(at == NX - 1, 0.0, pltpu.roll(here_f, NX - 1, 1))
             grad_z = field[r0 + 1 : r0 + 17, :] - field[r0 - 1 : r0 + 15, :]
             u, v, w = [vel[j, r : r + 16, :].astype(F32) for j in range(3)]
-            advection = u * ((high - low) * spacing[...])
+            advection = u * ((high - low) * scale[0:1, :])
             advection += 0.5 * (v * diff[r : r + 16, :]) + 0.5 * (w * grad_z)
             right[r : r + 16, :] = here_f - advection
         end = None
@@ -288,52 +459,73 @@
                 y = y + coef[k : k + 1, :] * head
                 solved[rows, B * k : B * (k + 1)] = y
             head = y[:, 0:1]
+        out_at = per_out * chunk
         for p in range(NQ):
-            for b in range(tout):
-                value = jnp.zeros((size, B), F32)
-                for t in quad_tiles(p, most_out):
-                    if t % tout == b:
-                        value = jnp.where(
-                            covers(begins_out, p, t), solved[rows, B * t : B * (t + 1)], value
-                        )
-                packed[p, rows, B * b : B * (b + 1)] = value
+            limit = jnp.minimum(begins_out[p] + RING, begins_out[p + 1])
+            values = [jnp.zeros((size, B), F32) for _ in range(2)]
+            rest = jnp.zeros((size, B), F32)
+            for t in quad_tiles(p, most):
+                tile = solved[rows, B * t : B * (t + 1)]
+                values[t % 2] = jnp.where(covers(begins_out[p], limit, t), tile, values[t % 2])
+                if wide_out:
+                    rest = jnp.where(covers(limit, begins_out[p + 1], t), tile, rest)
+            for b in range(2):
+                packed[p, out_at + size * b : out_at + size * (b + 1), :] = values[b]
+            if wide_out:
+                rest = rest + pltpu.roll(rest, B // 2, 1)
+                rest = rest + pltpu.roll(rest, B // 4, 1)
+                tight = rest[2 * REST : 3 * REST]
+                for g in (1, 0):
+                    tight = jnp.where(group16 == g, rest[REST * g : REST * (g + 1)], tight)
+                packed[p, out_at + 2 * size : out_at + 2 * size + REST, :] = tight
         for s in range(NQ - 1, 0, -1):
             to_q = (q + s) % NQ
             cp = remote(
-                packed.at[to_q, rows], rz.at[q, rows],
+                packed.at[to_q, pl.ds(out_at, per_out)], rz.at[q, pl.ds(out_at, per_out)],
                 z_send.at[chunk, s], z_recv.at[chunk, s], QX * to_q + x, c,
             )
             cp.start()
             z_copies[chunk, s] = cp
 
-    pieces = []
+    pieces, rests = [], []
+    limit = start_at(counts_out, QX * q) + RING
     for i in range(QX):
         at_row = QX * q + (x + i) % QX
-        pieces.append(slot_masks(tout, start_at(counts_out, at_row), counts_out[at_row], lane))
+        begin, count = start_at(counts_out, at_row), counts_out[at_row]
+        inner = jnp.minimum(jnp.maximum(limit - begin, 0), count)
+        pieces.append(slot_masks(2, begin, inner, lane))
+        rests.append(slot_masks(1, begin + inner, count - inner, lane)[0])
     y_copies = []
     for chunk, (first, size) in enumerate(CHUNKS):
+        out_at = per_out * chunk
         for s in range(NQ):
             from_q = (q + NQ - s) % NQ
             if s:
                 z_copies[chunk, s].wait_recv()
 
             def step(j, carry):
-                at_rows = pl.ds(pl.multiple_of(first + 8 * j, 8), 8)
-                if s:
-                    parts = [rz[from_q, at_rows, B * t : B * (t + 1)] for t in range(tout)]
-                else:
-                    parts = [packed[q, at_rows, B * t : B * (t + 1)] for t in range(tout)]
-                for d in range(QX):
-                    value = jnp.zeros((8, B), F32)
-                    for t in range(tout):
-                        value = jnp.where(pieces[d][t], parts[t], value)
-                    piece[d, s, at_rows, :] = value
+                r = pl.multiple_of(8 * j, 8)
+
+                def read(to):
+                    if s:
+                        return rz[from_q, pl.ds(out_at + to + r, 8), :]
+                    return packed[q, pl.ds(out_at + to + r, 8), :]
+
+                for g in range(size // REST):
+                    parts = [read(REST * g), read(size + REST * g)]
+                    if wide_out:
+                        rest = jnp.where(group == g, read(2 * size), 0.0)
+                        rest = rest + pltpu.roll(rest, B // 2, 1)
+                        parts.append(rest + pltpu.roll(rest, B // 4, 1))
+                    for d in range(QX):
+                        masks = pieces[d] + ([rests[d]] if wide_out else [])
+                        piece[d, s, pl.ds(first + REST * g + r, 8), :] = choose(masks, parts)
                 return carry
 
-            lax.fori_loop(0, size // 8, step, 0)
+            lax.fori_loop(0, REST // 8, step, 0)
             to = pl.multiple_of(ZL * (QX * from_q + x) + first, 8)
             for d in range(QX):
-                part, goal = piece.at[d, s, first : first + size], out.at[pl.ds(to, size), :]
+                part, goal = piece.at[d, s, pl.ds(first, size)], out.at[pl.ds(to, size), :]
                 if d:
                     cp = remote(
                         part, goal, y_send.at[chunk, d, s], y_recv.at[chunk, d, s],
@@ -355,40 +547,48 @@
     for s in range(NQ):
         for cp in x_copies[s][1:]:
             cp.wait_send()
-
-
-def flow(tin, tout, cid, counts_in, counts_out, link, turned, vel, spacing, inverse):
+        if even:
+            pl.when(q < NQ - 1)(n_copies[0, s].wait_send)
+            pl.when(q > 0)(n_copies[1, s].wait_send)
+
+
+def flow(even, wide_out, cid, counts_in, counts_out, link, turned, vel, spacing, inverse):
     dma = pltpu.SemaphoreType.DMA
     vmem = pl.BlockSpec(memory_space=pltpu.VMEM)
     smem = pl.BlockSpec(memory_space=pltpu.SMEM)
     hbm = pl.BlockSpec(memory_space=pl.ANY)
-    rows = ZL + HALO
     per = dma((NC, NQ))
+    lay = EVEN if even else WIDE
+    per_out = NC * (2 * 48 + (REST if wide_out else 0))
     return pl.pallas_call(
-        functools.partial(flow_kernel, tin, tout),
-        name="flow%d%d" % (tin, tout),
+        functools.partial(flow_kernel, even, wide_out),
+        name="flow%d%d" % (even, wide_out),
         out_shape=jax.ShapeDtypeStruct((KZ * B, B), F32),
         in_specs=[smem, smem, smem, vmem, hbm, vmem, hbm],
         out_specs=hbm,
         scratch_shapes=[
-            pltpu.VMEM((QX, NQ, ZL + 2 * HALO, B), F32),
-            pltpu.VMEM((NQ, rows, tin * B), F32),
-            pltpu.VMEM((NQ, rows, tin * B), F32),
-            pltpu.VMEM((NQ, ZL, tin * B), F32),
-            pltpu.VMEM((NQ, ZL, tin * B), F32),
+            pltpu.VMEM((QX, NQ, SPAN, B), F32),
+            pltpu.VMEM((NQ, lay.halo + lay.total, B), F32),
+            pltpu.VMEM((NQ, lay.halo + lay.total, B), F32),
+            pltpu.VMEM((NQ, lay.total, B), F32),
+            pltpu.VMEM((NQ, lay.total, B), F32),
+            pltpu.VMEM((2, NQ, SPAN, B), F32),
+            pltpu.VMEM((2, NQ, SPAN, B), F32),
             pltpu.VMEM((3, ZL, NX), jnp.bfloat16),
             pltpu.VMEM((KX, B, B), F32),
-            pltpu.VMEM((ZL + 2 * HALO, NX), F32),
+            pltpu.VMEM((SPAN, NX), F32),
             pltpu.VMEM((HALO, NX), F32),
             pltpu.VMEM((ZL, NX), F32),
             pltpu.VMEM((ZL, NX), F32),
             pltpu.VMEM((ZL, NX), F32),
             pltpu.VMEM((KX + 4, B), F32),
-            pltpu.VMEM((NQ, ZL, tout * B), F32),
-            pltpu.VMEM((NQ, ZL, tout * B), F32),
+            pltpu.VMEM((HALO, NX), F32),
+            pltpu.VMEM((NQ, per_out, B), F32),
+            pltpu.VMEM((NQ, per_out, B), F32),
             pltpu.VMEM((QX, NQ, ZL, B), F32),
             dma((2,)), dma((QX, NQ)), dma((QX, NQ)), dma((NQ,)),
-            per, per, dma((NC,)), per, per, per, per, per, per,
+            per, per, dma((NC,)), per, per, per, per,
+            dma((2, NQ)), dma((2, NQ)), per, per,
             dma((NC, QX, NQ)), dma((NC, QX, NQ)), per,
         ],
         compiler_params=pltpu.CompilerParams(
@@ -428,24 +628,25 @@
     vmem = pl.BlockSpec(memory_space=pltpu.VMEM)
     smem = pl.BlockSpec(memory_space=pltpu.SMEM)
     local = pltpu.CompilerParams(vmem_limit_bytes=LIMIT)
-    turned = pl.pallas_call(
+    turned, pick = pl.pallas_call(
         turn_kernel,
         name="turn",
-        out_shape=jax.ShapeDtypeStruct((KZ * B + 2 * HALO, B), F32),
-        in_specs=[smem, vmem],
-        out_specs=vmem,
+        out_shape=(
+            jax.ShapeDtypeStruct((KZ * B + 2 * HALO, B), F32),
+            jax.ShapeDtypeStruct((1,), jnp.int32),
+        ),
+        in_specs=[smem, smem, vmem],
+        out_specs=(vmem, smem),
         compiler_params=local,
-    )(counts_in, temp_in.reshape(SLOTS * KZ, B))
-    sums = jnp.sum(jnp.stack([counts_in, counts_out]).reshape(2, NQ, QX), axis=2)
-    wide = (jnp.max(sums, axis=1) > 2 * B).astype(jnp.int32)
+    )(counts_in, counts_out, temp_in.reshape(SLOTS * KZ, B))
     lines = lax.switch(
-        2 * wide[0] + wide[1],
+        pick[0],
         [
-            functools.partial(flow, tin, tout, 1 + i)
-            for i, (tin, tout) in enumerate(((2, 2), (2, 3), (3, 2), (3, 3)))
+            functools.partial(flow, even, wide_out, 1 + i)
+            for i, (even, wide_out) in enumerate(((1, 0), (1, 1), (0, 1)))
         ],
         counts_in, counts_out, link_x, turned,
-        velocity.reshape(3, ZL, NX), spacing_x.reshape(1, NX), inverse_x,
+        velocity.reshape(3, ZL, NX), spacing_x.reshape(KX, B), inverse_x,
     )
     out = pl.pallas_call(
         last_kernel,

time: 238 us -> 215 us (0.903)
  the two profiles are of different devices: /device:TPU:1 before, /device:TPU:136 now
where the time goes in v3:
time: 215 us
  Pallas kernels  212 us (99%)
    pallas_call x1, Pallas kernels, flow(): pl.pallas_call(functools.partial(flow_kernel, even, wide_out), name='flow...  203 us
    pallas_call x1, Pallas kernels, on_device(): pl.pallas_call(last_kernel, name='last', out_shape=jax.ShapeDtypeStruct((...  7 us

profile of v3, /device:TPU:136, one launch (start us, length us, event | category | flops | bytes accessed | tf_op | source)
XLA Modules:
  0.0 214.6 jit_solution(16314534241420382718)
XLA Ops:
  0.0 0.0 copy-start.1
  0.0 1.3 copy-done.1
  1.3 2.0 turn.1
  4.0 0.0 copy-start
  4.0 0.0 copy-start.2
  4.0 203.5 %conditional.1 = (f32[4608,128]{1,0:T(8,128)}) conditional(s32[]{:T(128)} %bitcast.1, (s32[32]{0:T(128)}, s32[32]{0:T(128)}, f32[11]{0:T(128)}, f32[4624,128]{1,0:T(8,128)S(1)}, bf16[3,144,1536]{2,1,0:T(8,128)(2,1)}, /*index=5*/f32[12,128]{1,0:T(8,128)}, f32[12,128,128]{2,1,0:T(8,128)}) %tuple.21, (s32[32]{0:T(128)}, s32[32]{0:T(128)}, ...), branch_computations={%region_0.0_spmd, %region_1.0_spmd, %region_2.0_spmd} | conditional | bytes 8 | solution.py:642
  4.2 202.8 %flow11.1 = f32[4608,128]{1,0:T(8,128)} custom-call(s32[32]{0:T(128)} %get-tuple-element.58.counts_in, s32[32]{0:T(128)} %get-tuple-element.59.counts_out, f32[11]{0:T(128)} %get-tuple-element.60.link, f32[4624,128]{1,0:T(8,128)S(1)} %get-tuple-element.61.turned, bf16[3,144,1536]{2,1,0:T(8,128)(2,1)} %get-tuple-element.62.vel_hbm, ...), custom_call_target="tpu_custom_call" | custom-call | tf_op jit(solution)/shard_map/cond/branch_1_fun/flow11/pallas_call | solution.py:563
  207.5 0.0 copy-done
  207.5 0.0 copy-done.2
  207.6 7.0 %last.1 = f32[2592,128]{1,0:T(8,128)} custom-call(s32[32]{0:T(128)} %counts.1, f32[35]{0:T(128)S(1)} %copy-done.2, f32[4608,128]{1,0:T(8,128)} %get-tuple-element.76.lines, f32[36,128,128]{2,1,0:T(8,128)S(1)} %copy-done), custom_call_target="tpu_custom_call" | custom-call | tf_op jit(solution)/shard_map/last/pallas_call | solution.py:651
Async XLA Ops:
  0.0 1.3 copy-start.1
  4.0 203.6 %copy-start = (f32[36,128,128]{2,1,0:T(8,128)S(1)}, f32[36,128,128]{2,1,0:T(8,128)}, u32[]{:S(2)}) copy-start(f32[36,128,128]{2,1,0:T(8,128)} %inverse.1) | copy-start | bytes 7077892
  4.0 203.6 %copy-start.2 = (f32[35]{0:T(128)S(1)}, f32[35]{0:T(128)}, u32[]{:S(2)}) copy-start(f32[35]{0:T(128)} %link.1) | copy-start | bytes 424

commit v4 on v3

--- a/solution.py
+++ b/solution.py
@@ -20,9 +20,12 @@
 SPAN = ZL + 2 * HALO
 RING = 256
 REST = 16
+PARTS = 6
 NX = KX * B
-CHUNKS = ((0, 48), (48, 48), (96, 48))
+CHUNKS = ((0, 64), (64, 48), (112, 32))
+STEPS = ((0, 48), (48, 48), (96, 48))
 NC = len(CHUNKS)
+MAIN = 2 * HALO
 F32 = jnp.float32
 LIMIT = 48 * 2**20
 
@@ -47,24 +50,13 @@
     return total
 
 
-def turn_kernel(counts_in, counts_out, temp, out, pick):
-    q, x, _ = here()
-    shift = start_at(counts_in, QX * q + x) % B
-    starts = starts_of(counts_in)
+def pick_kernel(counts_in, counts_out, pick):
+    starts, ends = starts_of(counts_in), starts_of(counts_out)
     drift, most = jnp.int32(0), jnp.int32(0)
-    ends = starts_of(counts_out)
     for p in range(NQ):
         drift = jnp.maximum(drift, jnp.abs(starts[QX * p] - QUAD * p))
         most = jnp.maximum(most, ends[QX * (p + 1)] - ends[QX * p])
     pick[0] = jnp.where(drift > B, 2, jnp.where(most > RING, 1, 0))
-    pad = jnp.zeros((B - SLOTS, B), F32)
-    for k in range(KZ):
-        block = temp[pl.ds(k, SLOTS, stride=KZ), :]
-        turned = jnp.concatenate([block, pad], axis=0).T
-        out[HALO + B * k : HALO + B * (k + 1), :] = pltpu.roll(turned, shift, 1)
-    total = KZ * B
-    out[0:HALO, :] = out[total : total + HALO, :]
-    out[total + HALO : total + 2 * HALO, :] = out[HALO : 2 * HALO, :]
 
 
 def across(c):
@@ -77,7 +69,7 @@
         pl.semaphore_signal(
             sem, inc=1, device_id={"row": row, "col": col}, device_id_type=MESH
         )
-    pl.semaphore_wait(sem, len(partners))
+    return lambda: pl.semaphore_wait(sem, len(partners))
 
 
 def remote(src, dst, send, recv, row, col):
@@ -92,7 +84,7 @@
 
 
 ORDER = (4, 3, 5, 2, 6, 1, 7, 0)
-LAG = 2
+LAG = 4
 
 
 def quad_tiles(q, most):
@@ -115,16 +107,16 @@
 
 
 class Layout:
-    def __init__(self, per_row, halo):
+    def __init__(self, per_two, rest, halo):
         self.halo = halo
-        self.rows = [size * per_row // 2 for _, size in CHUNKS]
+        self.rows = [size * per_two // 2 + rest for _, size in CHUNKS]
         self.at = [sum(self.rows[:i]) for i in range(NC)]
         self.total = sum(self.rows)
 
     def own(self, chunk):
         if chunk == 0:
             return pl.ds(0, self.halo + self.rows[0])
-        return pl.ds(self.halo + self.at[chunk], self.rows[chunk])
+        return self.inner(chunk)
 
     def inner(self, chunk):
         return pl.ds(self.halo + self.at[chunk], self.rows[chunk])
@@ -133,13 +125,13 @@
         return pl.ds(self.at[chunk], self.rows[chunk])
 
 
-EVEN = Layout(3, HALO)
-WIDE = Layout(6, 3 * HALO)
+EVEN = Layout(3, 0, HALO)
+WIDE = Layout(4, REST, 3 * HALO)
 
 
 def flow_kernel(
-    even, wide_out, counts_in, counts_out, link, turned, vel_hbm, spacing, inv_hbm, out,
-    xin, merged, own, cross, mate, away, come, vel, inverse, field, edge, diff, right, solved,
+    even, wide_out, counts_in, counts_out, link, temp_hbm, vel_hbm, spacing, inv_hbm, out,
+    temp, doubled, turned, xin, merged, own, cross, mate, away, come, vel, inverse, field, edge, diff, right, solved,
     coef, scale, packed, rz, piece,
     load, x_send, x_recv, x_local, o_send, o_recv, o_local, c_send, c_recv, m_send, m_recv,
     n_send, n_recv, z_send, z_recv, y_send, y_recv, y_local,
@@ -149,8 +141,9 @@
     other, twin = across(c), c + 1 - 2 * (c % 2)
     row = QX * q + x
     loads = [
-        pltpu.make_async_copy(vel_hbm, vel, load.at[0]),
-        pltpu.make_async_copy(inv_hbm, inverse, load.at[1]),
+        pltpu.make_async_copy(temp_hbm, temp, load.at[0]),
+        pltpu.make_async_copy(vel_hbm, vel, load.at[1]),
+        pltpu.make_async_copy(inv_hbm, inverse, load.at[2]),
     ]
     for cp in loads:
         cp.start()
@@ -158,32 +151,55 @@
     partners += [(QX * ((q + s) % NQ) + x, c) for s in range(1, NQ)]
     partners += [(QX * ((q + s) % NQ) + x, other) for s in range(NQ)]
     partners += [(row, twin)]
-    barrier(partners)
-
-    def source(to_q, to_x):
+    ready = barrier(partners)
+    loads[0].wait()
+    back = B - start_at(counts_in, row) % B
+    for j in range(2):
+        doubled[j, SLOTS:B, :] = jnp.zeros((B - SLOTS, B), F32)
+        doubled[j, B + SLOTS : 2 * B, :] = jnp.zeros((B - SLOTS, B), F32)
+    for k in range(KZ):
+        block, j = temp[pl.ds(k, SLOTS, stride=KZ), :], k % 2
+        doubled[j, 0:SLOTS, :] = block
+        doubled[j, B : B + SLOTS, :] = block
+        turned[HALO + B * k : HALO + B * (k + 1), :] = doubled[j, pl.ds(back, B), :].T
+    total = KZ * B
+    turned[0:HALO, :] = turned[total : total + HALO, :]
+    turned[total + HALO : total + 2 * HALO, :] = turned[HALO : 2 * HALO, :]
+    ready()
+
+    def parts_of(to_q, to_x, chunk):
         start = pl.multiple_of(QX * ZL * to_q + ZL * to_x, 8)
-        return turned.at[pl.ds(start, SPAN), :]
+        first, size = CHUNKS[chunk]
+        if chunk:
+            return [(start + HALO + first, MAIN + first, size)]
+        return [(start, HALO, HALO + size), (start + HALO + ZL, 0, HALO)]
 
     x_copies = {}
-    for s in ORDER:
-        to_q = (q + s) % NQ
-        local = pltpu.make_async_copy(source(to_q, x), xin.at[x, s], x_local.at[s])
-        local.start()
-        x_copies[s] = [local]
-        for d in range(1, QX):
-            to_x = (x + d) % QX
-            cp = remote(
-                source(to_q, to_x), xin.at[x, s], x_send.at[d, s], x_recv.at[d, s],
-                QX * q + to_x, c,
-            )
-            cp.start()
-            x_copies[s].append(cp)
+    for chunk in range(NC):
+        for s in ORDER:
+            to_q = (q + s) % NQ
+            copies = []
+            for d in range(QX):
+                to_x = (x + d) % QX
+                for n, (at_row, to_row, size) in enumerate(parts_of(to_q, to_x, chunk)):
+                    src = turned.at[pl.ds(at_row, size), :]
+                    dst = xin.at[x, s, pl.ds(to_row, size), :]
+                    sem = chunk + NC * n
+                    if d:
+                        cp = remote(
+                            src, dst, x_send.at[sem, d, s], x_recv.at[sem, d, s],
+                            QX * q + to_x, c,
+                        )
+                    else:
+                        cp = pltpu.make_async_copy(src, dst, x_local.at[sem, s])
+                    cp.start()
+                    copies.append((d, cp))
+            x_copies[chunk, s] = copies
 
     lane = lax.broadcasted_iota(jnp.int32, (8, B), 1)
     sub = lax.broadcasted_iota(jnp.int32, (8, B), 0)
-    edge_rows = [-1, ZL] + [first + size for first, size in CHUNKS[:-1]]
-    quad_first = start_at(counts_in, QX * q)
-    firsts = [quad_first]
+    group = lane // 32
+    firsts = [start_at(counts_in, QX * q)]
     for i in range(QX):
         firsts.append(firsts[-1] + counts_in[QX * q + i])
 
@@ -193,16 +209,20 @@
             value = jnp.where(mask, part, value)
         return value
 
-    def arrived(s):
-        x_copies[s][0].wait()
-        for cp in x_copies[s][1:]:
-            cp.wait_recv()
-
-    def edge_parts(s, rows, read):
-        value = jnp.zeros((8, B), F32)
-        for n, z in rows:
-            value = jnp.where(sub == n, read(z), value)
-        return value
+    def fold(value):
+        value = value + pltpu.roll(value, B // 2, 1)
+        return value + pltpu.roll(value, B // 4, 1)
+
+    def arrived(chunk, s):
+        for d, cp in x_copies[chunk, s]:
+            if d:
+                cp.wait_recv()
+            else:
+                cp.wait()
+
+    def edge_tile(read):
+        low, high = read(MAIN - 1), read(0)
+        return jnp.where(sub % 4 == 0, low, high)
 
     n_copies = {}
     if even:
@@ -223,96 +243,108 @@
             turn = (base + B) % B
             window_masks.append(inside(lane + (base - turn) + jnp.where(lane < turn, B, 0)))
 
-        def prepare(s):
-            arrived(s)
+        def prepare(chunk, s):
+            arrived(chunk, s)
+            first, size = CHUNKS[chunk]
+            low = 0 if chunk == 0 else MAIN + first
+            span = MAIN + first + size - low
 
             def step(j, carry):
-                rows = pl.ds(pl.multiple_of(8 * j, 8), 8)
+                rows = pl.ds(pl.multiple_of(low + 8 * j, 8), 8)
                 parts = [xin[i, s, rows, :] for i in range(QX)]
                 for side in range(2):
                     away[side, s, rows, :] = choose(window_masks[side], parts)
                 return carry
 
-            lax.fori_loop(0, SPAN // 8, step, 0)
+            lax.fori_loop(0, span // 8, step, 0)
             to_q = (q + s) % NQ
             for side, (inner, to) in enumerate(((q < NQ - 1, q + 1), (q > 0, q - 1))):
                 to = (to + NQ) % NQ
                 cp = remote(
-                    away.at[side, s], come.at[side, to_q],
-                    n_send.at[side, to_q], n_recv.at[side, to_q], QX * to + x, c,
+                    away.at[side, s, pl.ds(low, span), :],
+                    come.at[side, to_q, pl.ds(low, span), :],
+                    n_send.at[side, chunk, to_q], n_recv.at[side, chunk, to_q],
+                    QX * to + x, c,
                 )
-                n_copies[side, s] = cp
+                n_copies[side, chunk, s] = cp
                 pl.when(inner)(cp.start)
 
-        def merge(s):
+        def merge(chunk, s):
             to_q = (q + s) % NQ
-            pl.when(q > 0)(n_copies[0, s].wait_recv)
-            pl.when(q < NQ - 1)(n_copies[1, s].wait_recv)
+            pl.when(q > 0)(n_copies[0, chunk, s].wait_recv)
+            pl.when(q < NQ - 1)(n_copies[1, chunk, s].wait_recv)
 
             def parts_at(rows):
                 parts = [xin[i, s, rows, :] for i in range(QX)]
                 return parts + [come[side, to_q, rows, :] for side in range(2)]
 
-            for chunk, (first, size) in enumerate(CHUNKS):
-                base = lay.halo + lay.at[chunk]
-
-                def step(j, carry):
-                    r = pl.multiple_of(8 * j, 8)
-                    halves = []
-                    for up in (0, size // 2):
-                        parts = parts_at(pl.ds(HALO + first + up + r, 8))
-                        merged[s, pl.ds(base + up + r, 8), :] = choose(full_masks, parts)
-                        halves.append(choose(half_masks, parts))
-                    merged[s, pl.ds(base + size + r, 8), :] = jnp.where(
-                        natural, halves[0], pltpu.roll(halves[1], B // 2, 1)
-                    )
-                    return carry
-
-                lax.fori_loop(0, size // 16, step, 0)
-            parts = []
-            for rows in (
-                [lambda z, i=i: xin[i, s, HALO + z : HALO + z + 1, :] for i in range(QX)]
-                + [lambda z, i=i: come[i, to_q, HALO + z : HALO + z + 1, :] for i in range(2)]
-            ):
-                pairs = [(n, z) for n, z in enumerate(edge_rows)]
-                parts.append(edge_parts(s, pairs + [(4 + n, z) for n, z in pairs], rows))
-            merged[s, 0:HALO, :] = jnp.where(
-                sub < 4, choose(full_masks, parts), choose(half_masks, parts)
-            )
+            first, size = CHUNKS[chunk]
+            base = lay.halo + lay.at[chunk]
+
+            def step(j, carry):
+                r = pl.multiple_of(8 * j, 8)
+                halves = []
+                for up in (0, size // 2):
+                    parts = parts_at(pl.ds(MAIN + first + up + r, 8))
+                    merged[s, pl.ds(base + up + r, 8), :] = choose(full_masks, parts)
+                    halves.append(choose(half_masks, parts))
+                merged[s, pl.ds(base + size + r, 8), :] = jnp.where(
+                    natural, halves[0], pltpu.roll(halves[1], B // 2, 1)
+                )
+                return carry
+
+            lax.fori_loop(0, size // 16, step, 0)
+            if chunk == 0:
+                parts = [
+                    edge_tile(lambda r, i=i: xin[i, s, r : r + 1, :]) for i in range(QX)
+                ]
+                parts += [
+                    edge_tile(lambda r, i=i: come[i, to_q, r : r + 1, :]) for i in range(2)
+                ]
+                merged[s, 0:HALO, :] = jnp.where(
+                    sub < 4, choose(full_masks, parts), choose(half_masks, parts)
+                )
 
     else:
-        takes = [
-            slot_masks(3, firsts[i], firsts[i + 1] - firsts[i], lane) for i in range(QX)
-        ]
-
-        def prepare(s):
-            arrived(s)
-
-        def merge(s):
-            for chunk, (first, size) in enumerate(CHUNKS):
-                base = lay.halo + lay.at[chunk]
-
-                def step(j, carry):
-                    r = pl.multiple_of(8 * j, 8)
-                    parts = [xin[i, s, pl.ds(HALO + first + r, 8), :] for i in range(QX)]
-                    for t in range(3):
-                        merged[s, pl.ds(base + t * size + r, 8), :] = choose(
+        limit_in = firsts[0] + RING
+        takes, rest_takes = [], []
+        for i in range(QX):
+            count = firsts[i + 1] - firsts[i]
+            inner = jnp.minimum(jnp.maximum(limit_in - firsts[i], 0), count)
+            takes.append(slot_masks(2, firsts[i], inner, lane))
+            rest_takes.append(slot_masks(1, firsts[i] + inner, count - inner, lane)[0])
+
+        def prepare(chunk, s):
+            arrived(chunk, s)
+
+        def merge(chunk, s):
+            first, size = CHUNKS[chunk]
+            base = lay.halo + lay.at[chunk]
+
+            def step(j, carry):
+                r = pl.multiple_of(8 * j, 8)
+                tight = jnp.zeros((8, B), F32)
+                for g in range(size // REST):
+                    at_row = REST * g + r
+                    parts = [xin[i, s, pl.ds(MAIN + first + at_row, 8), :] for i in range(QX)]
+                    for t in range(2):
+                        merged[s, pl.ds(base + t * size + at_row, 8), :] = choose(
                             [takes[i][t] for i in range(QX)], parts
                         )
-                    return carry
-
-                lax.fori_loop(0, size // 8, step, 0)
-            parts = [
-                edge_parts(
-                    s, list(enumerate(edge_rows)),
-                    lambda z, i=i: xin[i, s, HALO + z : HALO + z + 1, :],
-                )
-                for i in range(QX)
-            ]
-            for t in range(3):
-                merged[s, HALO * t : HALO * (t + 1), :] = choose(
-                    [takes[i][t] for i in range(QX)], parts
-                )
+                    tight = jnp.where(group == g, fold(choose(rest_takes, parts)), tight)
+                merged[s, pl.ds(base + 2 * size + r, 8), :] = tight
+                return carry
+
+            lax.fori_loop(0, REST // 8, step, 0)
+            if chunk == 0:
+                parts = [
+                    edge_tile(lambda r, i=i: xin[i, s, r : r + 1, :]) for i in range(QX)
+                ]
+                for t in range(2):
+                    merged[s, HALO * t : HALO * (t + 1), :] = choose(
+                        [takes[i][t] for i in range(QX)], parts
+                    )
+                merged[s, 2 * HALO : 3 * HALO, :] = fold(choose(rest_takes, parts))
 
     def send_rows(s, chunk):
         to_q = (q + s) % NQ
@@ -333,15 +365,13 @@
 
     o_copies, c_copies = {}, {}
     lag = LAG if even else 0
-    for n in range(NQ + lag):
-        if n < NQ:
-            prepare(ORDER[n])
+    todo = [(chunk, s) for chunk in range(NC) for s in ORDER]
+    for n in range(len(todo) + lag):
+        if n < len(todo):
+            prepare(*todo[n])
         if n >= lag:
-            s = ORDER[n - lag]
-            merge(s)
-            o_copies[0, s], c_copies[0, s] = send_rows(s, 0)
-    for chunk in range(1, NC):
-        for s in ORDER:
+            chunk, s = todo[n - lag]
+            merge(chunk, s)
             o_copies[chunk, s], c_copies[chunk, s] = send_rows(s, chunk)
 
     line = lax.broadcasted_iota(jnp.int32, (1, B), 1)
@@ -355,12 +385,24 @@
 
     def assemble(dst, to, size, read):
         if not even:
+            rests = []
+            for p in range(NQ):
+                if size == HALO:
+                    rests.append(read(p, 2 * size, HALO))
+                    continue
+                tight = read(p, 2 * size, REST)
+                groups = [
+                    fold(jnp.where(group16 == g, tight, 0.0)) for g in range(size // REST)
+                ]
+                rests.append(jnp.concatenate(groups, axis=0))
             for t in range(KX):
                 value = jnp.zeros((size, B), F32)
                 for p in range(NQ):
                     if t in quad_tiles(p, most):
-                        mask = covers(begins_in[p], begins_in[p + 1], t)
-                        value = jnp.where(mask, read(p, size * (t % 3), size), value)
+                        limit = jnp.minimum(begins_in[p] + RING, begins_in[p + 1])
+                        part = read(p, size * (t % 2), size)
+                        value = jnp.where(covers(begins_in[p], limit, t), part, value)
+                        value = jnp.where(covers(limit, begins_in[p + 1], t), rests[p], value)
                 dst[to : to + size, B * t : B * (t + 1)] = value
             return
         h = size // 2
@@ -390,11 +432,10 @@
         scale[0:1, B * t : B * (t + 1)] = spacing[t : t + 1, :]
     at = lax.broadcasted_iota(jnp.int32, (16, NX), 1)
     per_out = 2 * 48 + (REST if wide_out else 0)
-    group = lane // 32
     group16 = lax.broadcasted_iota(jnp.int32, (REST, B), 1) // 32
     z_copies, m_copies = {}, {}
     for chunk, (first, size) in enumerate(CHUNKS):
-        for s in range(NQ):
+        for s in ORDER:
             from_q = (q + NQ - s) % NQ
             if s:
                 o_copies[chunk, s].wait_recv()
@@ -409,16 +450,13 @@
         if chunk == 0:
             assemble_edge()
             field[HALO - 1 : HALO, :] = edge[0:1, :]
-        rows = slice(first, first + size)
+            field[HALO + ZL : HALO + ZL + 1, :] = edge[1:2, :]
         o_at, c_at = lay.halo + lay.at[chunk], lay.at[chunk]
         assemble(
             field, first + HALO, size, lambda p, r, n: own[p, o_at + r : o_at + r + n, :]
         )
-        last = 1 if chunk == NC - 1 else 2 + chunk
-        after = first + HALO + size
-        field[after : after + 1, :] = edge[last : last + 1, :]
         if chunk == 0:
-            for cp in loads:
+            for cp in loads[1:]:
                 cp.wait()
         for s in range(NQ):
             c_copies[chunk, s].wait_recv()
@@ -429,6 +467,8 @@
                 mate[p, c_at + r : c_at + r + n, :] - cross[p, c_at + r : c_at + r + n, :]
             ) * sign,
         )
+        first, size = STEPS[chunk]
+        rows = slice(first, first + size)
         for r in range(first, first + size, 16):
             r0 = r + HALO
             here_f = field[r0 : r0 + 16, :]
@@ -472,13 +512,12 @@
             for b in range(2):
                 packed[p, out_at + size * b : out_at + size * (b + 1), :] = values[b]
             if wide_out:
-                rest = rest + pltpu.roll(rest, B // 2, 1)
-                rest = rest + pltpu.roll(rest, B // 4, 1)
+                rest = fold(rest)
                 tight = rest[2 * REST : 3 * REST]
                 for g in (1, 0):
                     tight = jnp.where(group16 == g, rest[REST * g : REST * (g + 1)], tight)
                 packed[p, out_at + 2 * size : out_at + 2 * size + REST, :] = tight
-        for s in range(NQ - 1, 0, -1):
+        for s in ORDER[:-1]:
             to_q = (q + s) % NQ
             cp = remote(
                 packed.at[to_q, pl.ds(out_at, per_out)], rz.at[q, pl.ds(out_at, per_out)],
@@ -496,9 +535,9 @@
         pieces.append(slot_masks(2, begin, inner, lane))
         rests.append(slot_masks(1, begin + inner, count - inner, lane)[0])
     y_copies = []
-    for chunk, (first, size) in enumerate(CHUNKS):
+    for chunk, (first, size) in enumerate(STEPS):
         out_at = per_out * chunk
-        for s in range(NQ):
+        for s in (0,) + ORDER[:-1]:
             from_q = (q + NQ - s) % NQ
             if s:
                 z_copies[chunk, s].wait_recv()
@@ -514,9 +553,7 @@
                 for g in range(size // REST):
                     parts = [read(REST * g), read(size + REST * g)]
                     if wide_out:
-                        rest = jnp.where(group == g, read(2 * size), 0.0)
-                        rest = rest + pltpu.roll(rest, B // 2, 1)
-                        parts.append(rest + pltpu.roll(rest, B // 4, 1))
+                        parts.append(fold(jnp.where(group == g, read(2 * size), 0.0)))
                     for d in range(QX):
                         masks = pieces[d] + ([rests[d]] if wide_out else [])
                         piece[d, s, pl.ds(first + REST * g + r, 8), :] = choose(masks, parts)
@@ -544,15 +581,16 @@
             if s:
                 o_copies[chunk, s].wait_send()
                 z_copies[chunk, s].wait_send()
-    for s in range(NQ):
-        for cp in x_copies[s][1:]:
-            cp.wait_send()
+    for chunk, s in todo:
+        for d, cp in x_copies[chunk, s]:
+            if d:
+                cp.wait_send()
         if even:
-            pl.when(q < NQ - 1)(n_copies[0, s].wait_send)
-            pl.when(q > 0)(n_copies[1, s].wait_send)
-
-
-def flow(even, wide_out, cid, counts_in, counts_out, link, turned, vel, spacing, inverse):
+            pl.when(q < NQ - 1)(n_copies[0, chunk, s].wait_send)
+            pl.when(q > 0)(n_copies[1, chunk, s].wait_send)
+
+
+def flow(even, wide_out, cid, counts_in, counts_out, link, temp, vel, spacing, inverse):
     dma = pltpu.SemaphoreType.DMA
     vmem = pl.BlockSpec(memory_space=pltpu.VMEM)
     smem = pl.BlockSpec(memory_space=pltpu.SMEM)
@@ -564,9 +602,12 @@
         functools.partial(flow_kernel, even, wide_out),
         name="flow%d%d" % (even, wide_out),
         out_shape=jax.ShapeDtypeStruct((KZ * B, B), F32),
-        in_specs=[smem, smem, smem, vmem, hbm, vmem, hbm],
+        in_specs=[smem, smem, smem, hbm, hbm, vmem, hbm],
         out_specs=hbm,
         scratch_shapes=[
+            pltpu.VMEM((SLOTS * KZ, B), F32),
+            pltpu.VMEM((2, 2 * B, B), F32),
+            pltpu.VMEM((KZ * B + 2 * HALO, B), F32),
             pltpu.VMEM((QX, NQ, SPAN, B), F32),
             pltpu.VMEM((NQ, lay.halo + lay.total, B), F32),
             pltpu.VMEM((NQ, lay.halo + lay.total, B), F32),
@@ -586,24 +627,31 @@
             pltpu.VMEM((NQ, per_out, B), F32),
             pltpu.VMEM((NQ, per_out, B), F32),
             pltpu.VMEM((QX, NQ, ZL, B), F32),
-            dma((2,)), dma((QX, NQ)), dma((QX, NQ)), dma((NQ,)),
+            dma((3,)), dma((NC + 1, QX, NQ)), dma((NC + 1, QX, NQ)), dma((NC + 1, NQ)),
             per, per, dma((NC,)), per, per, per, per,
-            dma((2, NQ)), dma((2, NQ)), per, per,
+            dma((2, NC, NQ)), dma((2, NC, NQ)), per, per,
             dma((NC, QX, NQ)), dma((NC, QX, NQ)), per,
         ],
         compiler_params=pltpu.CompilerParams(
             collective_id=cid, has_side_effects=True, vmem_limit_bytes=LIMIT
         ),
-    )(counts_in, counts_out, link, turned, vel, spacing, inverse)
-
-
-def last_kernel(counts, link, lines, inverse, out, solved):
+    )(counts_in, counts_out, link, temp, vel, spacing, inverse)
+
+
+def last_kernel(counts, link, lines_hbm, inverse, out, lines, solved, doubled, load):
     q, x, _ = here()
-    back = (B - start_at(counts, QX * q + x) % B) % B
-    count = counts[QX * q + x]
-    valid = lax.broadcasted_iota(jnp.int32, (SLOTS, B), 0) < count
+    row = QX * q + x
+    off = start_at(counts, row) % B
+    valid = lax.broadcasted_iota(jnp.int32, (SLOTS, B), 0) < counts[row]
+    parts = []
+    for n in range(PARTS):
+        rows = pl.ds(KZ * B // PARTS * n, KZ * B // PARTS)
+        parts.append(pltpu.make_async_copy(lines_hbm.at[rows], lines.at[rows], load.at[n]))
+        parts[n].start()
     end = None
     for k in range(KZ):
+        if k % (KZ // PARTS) == 0:
+            parts[k // (KZ // PARTS)].wait()
         y = jnp.dot(
             inverse[k], lines[B * k : B * (k + 1), :], precision=HIGH,
             preferred_element_type=F32,
@@ -618,8 +666,11 @@
         if k < KZ - 1:
             y = y + (link[k] * inverse[k, :, B - 1 : B]) * head
         head = y[0:1, :]
-        turned = pltpu.roll(y, back, 1).T
-        out[pl.ds(k, SLOTS, stride=KZ), :] = jnp.where(valid, turned[0:SLOTS, :], 0.0)
+        turned, j = y.T, k % 4
+        doubled[j, 0:B, :] = turned
+        doubled[j, B : B + SLOTS, :] = turned[0:SLOTS]
+        mine = doubled[j, pl.ds(off, SLOTS), :]
+        out[pl.ds(k, SLOTS, stride=KZ), :] = jnp.where(valid, mine, 0.0)
 
 
 def on_device(
@@ -628,33 +679,34 @@
     vmem = pl.BlockSpec(memory_space=pltpu.VMEM)
     smem = pl.BlockSpec(memory_space=pltpu.SMEM)
     local = pltpu.CompilerParams(vmem_limit_bytes=LIMIT)
-    turned, pick = pl.pallas_call(
-        turn_kernel,
-        name="turn",
-        out_shape=(
-            jax.ShapeDtypeStruct((KZ * B + 2 * HALO, B), F32),
-            jax.ShapeDtypeStruct((1,), jnp.int32),
-        ),
-        in_specs=[smem, smem, vmem],
-        out_specs=(vmem, smem),
-        compiler_params=local,
-    )(counts_in, counts_out, temp_in.reshape(SLOTS * KZ, B))
+    pick = pl.pallas_call(
+        pick_kernel,
+        name="pick",
+        out_shape=jax.ShapeDtypeStruct((1,), jnp.int32),
+        in_specs=[smem, smem],
+        out_specs=smem,
+    )(counts_in, counts_out)
     lines = lax.switch(
         pick[0],
         [
             functools.partial(flow, even, wide_out, 1 + i)
             for i, (even, wide_out) in enumerate(((1, 0), (1, 1), (0, 1)))
         ],
-        counts_in, counts_out, link_x, turned,
+        counts_in, counts_out, link_x, temp_in.reshape(SLOTS * KZ, B),
         velocity.reshape(3, ZL, NX), spacing_x.reshape(KX, B), inverse_x,
     )
     out = pl.pallas_call(
         last_kernel,
         name="last",
         out_shape=jax.ShapeDtypeStruct((SLOTS * KZ, B), F32),
-        in_specs=[smem, smem, vmem, vmem],
+        in_specs=[smem, smem, pl.BlockSpec(memory_space=pl.ANY), vmem],
         out_specs=vmem,
-        scratch_shapes=[pltpu.VMEM((KZ * B, B), F32)],
+        scratch_shapes=[
+            pltpu.VMEM((KZ * B, B), F32),
+            pltpu.VMEM((KZ * B, B), F32),
+            pltpu.VMEM((4, 2 * B, B), F32),
+            pltpu.SemaphoreType.DMA((PARTS,)),
+        ],
         compiler_params=local,
     )(counts_out, link_z, lines, inverse_z)
     return out.reshape(SLOTS, 1, KZ * B)

time: 215 us -> 203 us (0.944)
  the two profiles are of different devices: /device:TPU:136 before, /device:TPU:1 now
where the time goes in v4:
time: 203 us; the launch traced here: 202 us
  Pallas kernels  201 us (99%)
    pallas_call x1, Pallas kernels, flow(): pl.pallas_call(functools.partial(flow_kernel, even, wide_out), name='flow...  193 us
    pallas_call x1, Pallas kernels, on_device(): pl.pallas_call(last_kernel, name='last', out_shape=jax.ShapeDtypeStruct((...  6.14 us

profile of v4, /device:TPU:1, one launch (start us, length us, event | category | flops | bytes accessed | tf_op | source)
XLA Modules:
  0.0 202.4 jit_solution(8047692196304982570)
XLA Ops:
  0.0 1.2 pick.1
  1.9 0.0 copy-start
  1.9 0.0 copy-start.1
  1.9 194.1 %conditional.1 = (f32[4608,128]{1,0:T(8,128)}) conditional(s32[]{:T(128)} %bitcast, (s32[32]{0:T(128)}, s32[32]{0:T(128)}, f32[11]{0:T(128)}, f32[2592,128]{1,0:T(8,128)}, bf16[3,144,1536]{2,1,0:T(8,128)(2,1)}, /*index=5*/f32[12,128]{1,0:T(8,128)}, f32[12,128,128]{2,1,0:T(8,128)}) %tuple.24, (s32[32]{0:T(128)}, s32[32]{0:T(128)}, ...), branch_computations={%region_0.0_spmd, %region_1.0_spmd, %region_2.0_spmd} | conditional | bytes 8 | solution.py:689
  2.1 193.4 %flow11.1 = f32[4608,128]{1,0:T(8,128)} custom-call(s32[32]{0:T(128)} %get-tuple-element.58.counts_in, s32[32]{0:T(128)} %get-tuple-element.59.counts_out, f32[11]{0:T(128)} %get-tuple-element.60.link, f32[2592,128]{1,0:T(8,128)} %get-tuple-element.61.temp_hbm, bf16[3,144,1536]{2,1,0:T(8,128)(2,1)} %get-tuple-element.62.vel_hbm, ...), custom_call_target="tpu_custom_call" | custom-call | tf_op jit(solution)/shard_map/cond/branch_1_fun/flow11/pallas_call | solution.py:601
  196.0 0.0 copy-done
  196.0 0.0 copy-done.1
  196.0 6.1 %last.1 = f32[2592,128]{1,0:T(8,128)} custom-call(s32[32]{0:T(128)} %counts.1, f32[35]{0:T(128)S(1)} %copy-done.1, f32[4608,128]{1,0:T(8,128)} %get-tuple-element.72.lines_hbm, f32[36,128,128]{2,1,0:T(8,128)S(1)} %copy-done), custom_call_target="tpu_custom_call" | custom-call | tf_op jit(solution)/shard_map/last/pallas_call | solution.py:698
Async XLA Ops:
  1.9 194.1 %copy-start = (f32[36,128,128]{2,1,0:T(8,128)S(1)}, f32[36,128,128]{2,1,0:T(8,128)}, u32[]{:S(2)}) copy-start(f32[36,128,128]{2,1,0:T(8,128)} %inverse.1) | copy-start | bytes 7077892
  1.9 194.1 %copy-start.1 = (f32[35]{0:T(128)S(1)}, f32[35]{0:T(128)}, u32[]{:S(2)}) copy-start(f32[35]{0:T(128)} %link.1) | copy-start | bytes 424
